TPU v7x, 512 devices: a whole 4x8x8 slice. The times are simulated.
512 devices in a mesh: wide: 64 (over y, x, core), narrow: 8 (over z).
Axes of the slice: x: 4, y: 8, z: 8, core: 2. Of those that a mesh axis runs over, the one named last changes fastest.
Arguments:
- tokens: bfloat16 [256, 8192], P('wide', 'narrow'), may hold values from -6 to 6
- cotangent: bfloat16 [256, 8192], P('wide', 'narrow'), may hold values from -4 to 4
- rewards: float32 [256], P('wide'), may hold values from -6 to 6
- group_ids: int32 [256], P('wide'), may hold values from 0 to 15, never falling along the last dimension, each value on 1 to 32 neighbouring positions
- token_mask: int32 [256], P('wide'), may hold values 0 or 1
- w_gate: bfloat16 [8192, 32768], P('narrow', 'wide'), may hold values from -0.0625 to 0.0625
- w_up: bfloat16 [8192, 32768], P('narrow', 'wide'), may hold values from -0.0625 to 0.0625
- down_weight_frozen: bfloat16 [32768, 8192], P('wide', 'narrow'), may hold values from -0.03125 to 0.03125
- a_gate: bfloat16 [8192, 64], P('narrow'), may hold values from -0.0625 to 0.0625
- a_up: bfloat16 [8192, 64], P('narrow'), may hold values from -0.0625 to 0.0625
- gate_output_factor: bfloat16 [64, 32768], P(None, 'wide'), may hold values from -0.375 to 0.375
- up_output_factor: bfloat16 [64, 32768], P(None, 'wide'), may hold values from -0.375 to 0.375
- a_down: bfloat16 [32768, 64], P('wide'), may hold values from -0.03125 to 0.03125
- down_output_factor: bfloat16 [64, 8192], P(None, 'narrow'), may hold values from -0.375 to 0.375
Outputs:
- grad_x: bfloat16 [256, 8192], P('wide', 'narrow')
- divergence: float32 [256], P('wide')
- grad_a_gate: float32 [8192, 64], P('narrow')
- grad_a_up: float32 [8192, 64], P('narrow')
- gate_output_gradient: float32 [64, 32768], P(None, 'wide')
- up_output_gradient: float32 [64, 32768], P(None, 'wide')
- grad_a_down: float32 [32768, 64], P('wide')
- down_output_gradient: float32 [64, 8192], P(None, 'narrow')
Inputs may be any that keep to these rules, and one draw needn't show every extreme that they name: `group_ids`: group ids never fall along the tokens; each group holds 1 to 32 tokens.
All inputs are finite; a program needn't handle non-finite values. No bound on the sum of `token_mask` on one device may be relied on, other than what follows from the above.
Results may differ from a plain program's by a relative error of at most 0.035.
Values may be sent and summed in bfloat16 or wider, within the bound.
A program may use at most 64 MiB of HBM per device.

v0:
```python
import jax
import jax.numpy as jnp
from jax import lax
from jax.sharding import PartitionSpec as P

D = 8192
TOKENS = 256
GROUPS = 16


ADAPTER_SCALE = 2.0
KL_WEIGHT = 0.1


def frozen_product_rows(operand, weights):
    return jnp.dot(operand, weights, preferred_element_type=jnp.float32)


def trailing_inner_rows(operand, weights):
    return lax.dot_general(
        operand, weights, (((1,), (1,)), ((), ())), preferred_element_type=jnp.float32
    )


def leading_inner_rows(operand, weights):
    return lax.dot_general(
        operand, weights, (((0,), (0,)), ((), ())), preferred_element_type=jnp.float32
    )


def swish_parts(pre_gate):
    sigmoid = jax.nn.sigmoid(pre_gate)
    return (pre_gate * sigmoid, sigmoid * (1.0 + pre_gate * (1.0 - sigmoid)))


def forward_rows(
    gate_frozen_rows,
    up_frozen_rows,
    gate_adapter_factor,
    up_adapter_factor,
    gate_output_factor,
    up_output_factor,
):
    gate_policy_rows = gate_frozen_rows + ADAPTER_SCALE * frozen_product_rows(
        gate_adapter_factor, gate_output_factor
    )
    up_policy_rows = up_frozen_rows + ADAPTER_SCALE * frozen_product_rows(
        up_adapter_factor, up_output_factor
    )
    swish_policy, slope_policy = swish_parts(gate_policy_rows)
    swish_base, base_slope = swish_parts(gate_frozen_rows)
    policy_full = swish_policy * up_policy_rows
    hidden_policy = policy_full.astype(jnp.bfloat16)
    hidden_delta_rows = (policy_full - swish_base * up_frozen_rows).astype(jnp.bfloat16)
    return (up_policy_rows, swish_policy, slope_policy, hidden_policy, hidden_delta_rows)


def backward_rows(grad_hidden, up_policy_rows, swish_policy, slope_policy):
    gate_gradient_rows = (grad_hidden * up_policy_rows * slope_policy).astype(jnp.bfloat16)
    up_gradient_rows = (grad_hidden * swish_policy).astype(jnp.bfloat16)
    return (gate_gradient_rows, up_gradient_rows)


def shards(
    tokens,
    cotangent,
    rewards,
    group_ids,
    token_mask,
    w_gate,
    w_up,
    down_weight_frozen,
    a_gate,
    a_up,
    gate_output_factor,
    up_output_factor,
    a_down,
    down_output_factor,
):
    own_rows = tokens.shape[0]
    wide_begin = lax.axis_index("wide") * own_rows
    mask_float = token_mask.astype(jnp.float32)
    membership = (group_ids[:, None] == jnp.arange(GROUPS, dtype=jnp.int32)[None, :]).astype(
        jnp.float32
    )
    group_reward, group_count = lax.psum(
        (
            jnp.sum(membership * (mask_float * rewards)[:, None], axis=0),
            jnp.sum(membership * mask_float[:, None], axis=0),
        ),
        "wide",
    )
    group_mean = group_reward / jnp.maximum(group_count, 1.0)
    advantage = rewards - jnp.sum(membership * group_mean[None, :], axis=1)
    token_scale = mask_float * (TOKENS / jnp.maximum(jnp.sum(group_count), 1.0))
    gathered = lax.all_gather(tokens, "wide", axis=0, tiled=True)
    gate_part = frozen_product_rows(gathered, w_gate)
    up_part = frozen_product_rows(gathered, w_up)
    factor_gate_part = frozen_product_rows(gathered, a_gate)
    factor_up_part = frozen_product_rows(gathered, a_up)
    gate_frozen_rows, up_frozen_rows, factor_gate_sum, factor_up_sum = (
        lax.psum(gate_part.astype(jnp.bfloat16), "narrow").astype(jnp.float32),
        lax.psum(up_part.astype(jnp.bfloat16), "narrow").astype(jnp.float32),
        lax.psum(factor_gate_part.astype(jnp.bfloat16), "narrow").astype(jnp.float32),
        lax.psum(factor_up_part.astype(jnp.bfloat16), "narrow").astype(jnp.float32),
    )
    gate_adapter_factor = factor_gate_sum.astype(jnp.bfloat16)
    up_adapter_factor = factor_up_sum.astype(jnp.bfloat16)
    up_policy_rows, swish_policy, slope_policy, hidden_policy, hidden_delta_rows = forward_rows(
        gate_frozen_rows,
        up_frozen_rows,
        gate_adapter_factor,
        up_adapter_factor,
        gate_output_factor,
        up_output_factor,
    )
    down_adapter_factor = lax.psum(frozen_product_rows(hidden_policy, a_down), "wide").astype(
        jnp.bfloat16
    )
    local_down_adapter = lax.dynamic_slice_in_dim(down_adapter_factor, wide_begin, own_rows, 0)
    output_delta_rows = lax.psum_scatter(
        frozen_product_rows(hidden_delta_rows, down_weight_frozen),
        "wide",
        scatter_dimension=0,
        tiled=True,
    ) + ADAPTER_SCALE * frozen_product_rows(local_down_adapter, down_output_factor)
    divergence = (
        lax.psum(0.5 * jnp.sum(output_delta_rows * output_delta_rows, axis=1), "narrow") / D
    )
    output_gradient_rows = (
        token_scale[:, None]
        * (KL_WEIGHT * output_delta_rows - advantage[:, None] * cotangent.astype(jnp.float32))
    ).astype(jnp.bfloat16)
    down_output_slice = ADAPTER_SCALE * leading_inner_rows(local_down_adapter, output_gradient_rows)
    down_output_gradient = lax.psum(down_output_slice, "wide")
    adapter_gradient_slice = ADAPTER_SCALE * trailing_inner_rows(
        output_gradient_rows, down_output_factor
    )
    hidden_part = trailing_inner_rows(
        lax.all_gather(output_gradient_rows, "wide", axis=0, tiled=True), down_weight_frozen
    )
    factor_grad_rows = lax.all_gather(adapter_gradient_slice, "wide", axis=0, tiled=True)
    hidden_base, factor_grad_sum = (
        lax.psum(hidden_part.astype(jnp.bfloat16), "narrow").astype(jnp.float32),
        lax.psum(factor_grad_rows.astype(jnp.bfloat16), "narrow").astype(jnp.float32),
    )
    down_adapter_gradient = factor_grad_sum.astype(jnp.bfloat16)
    grad_hidden = hidden_base + trailing_inner_rows(down_adapter_gradient, a_down)
    gate_gradient_rows, up_gradient_rows = backward_rows(
        grad_hidden, up_policy_rows, swish_policy, slope_policy
    )
    grad_a_down = leading_inner_rows(hidden_policy, down_adapter_gradient)
    gate_output_gradient = ADAPTER_SCALE * leading_inner_rows(
        gate_adapter_factor, gate_gradient_rows
    )
    up_output_gradient = ADAPTER_SCALE * leading_inner_rows(up_adapter_factor, up_gradient_rows)
    gate_adapter_slice = ADAPTER_SCALE * trailing_inner_rows(gate_gradient_rows, gate_output_factor)
    up_adapter_slice = ADAPTER_SCALE * trailing_inner_rows(up_gradient_rows, up_output_factor)
    gate_factor_sum, up_factor_sum = lax.psum((gate_adapter_slice, up_adapter_slice), "wide")
    gate_adapter_gradient = gate_factor_sum.astype(jnp.bfloat16)
    up_adapter_gradient = up_factor_sum.astype(jnp.bfloat16)
    grad_a_gate = leading_inner_rows(gathered, gate_adapter_gradient)
    grad_a_up = leading_inner_rows(gathered, up_adapter_gradient)
    own_gate_factor = lax.dynamic_slice_in_dim(gate_adapter_gradient, wide_begin, own_rows, 0)
    own_up_factor = lax.dynamic_slice_in_dim(up_adapter_gradient, wide_begin, own_rows, 0)
    input_base = lax.psum_scatter(
        trailing_inner_rows(gate_gradient_rows, w_gate)
        + trailing_inner_rows(up_gradient_rows, w_up),
        "wide",
        scatter_dimension=0,
        tiled=True,
    )
    grad_x = (
        input_base
        + trailing_inner_rows(own_gate_factor, a_gate)
        + trailing_inner_rows(own_up_factor, a_up)
    ).astype(jnp.bfloat16)
    return (
        grad_x,
        divergence,
        grad_a_gate,
        grad_a_up,
        gate_output_gradient,
        up_output_gradient,
        grad_a_down,
        down_output_gradient,
    )


def solution(mesh):
    return jax.shard_map(
        shards,
        mesh=mesh,
        in_specs=(
            P("wide", "narrow"),
            P("wide", "narrow"),
            P("wide"),
            P("wide"),
            P("wide"),
            P("narrow", "wide"),
            P("narrow", "wide"),
            P("wide", "narrow"),
            P("narrow", None),
            P("narrow", None),
            P(None, "wide"),
            P(None, "wide"),
            P("wide", None),
            P(None, "narrow"),
        ),
        out_specs=(
            P("wide", "narrow"),
            P("wide"),
            P("narrow", None),
            P("narrow", None),
            P(None, "wide"),
            P(None, "wide"),
            P("wide", None),
            P(None, "narrow"),
        ),
        check_vma=False,
    )
```

profile of v0, /device:TPU:1, one launch (start us, length us, event | category | flops | bytes accessed | tf_op | source)
XLA Modules:
  0.0 906.0 jit_solution(3277044012381114689)
XLA Ops:
  7.2 54.5 %all-gather = bf16[64,4,1024]{2,1,0:T(4,128)(2,1)S(1)} all-gather(bf16[1,4,1024]{2,1,0:T(4,128)(2,1)} %bitcast.55), channel_id=1, replica_groups=mesh['wide'=64,'narrow'=8] {'wide'}, dimensions={0}, use_global_device_ids=true | all-gather | bytes 532480 | tf_op jit(solution)/shard_map/all_gather | solution.py:96
  63.9 1.1 convolution_convert_fusion.2
  65.1 1.2 convolution_convert_fusion.1
  67.0 1.3 dynamic-slice
  69.7 66.6 %all-reduce.20.cloned.1.call-done = (bf16[256,64]{0,1:T(8,128)(2,1)}, bf16[256,64]{0,1:T(8,128)(2,1)}) async-done(((bf16[256,64]{0,1:T(8,128)(2,1)}, bf16[256,64]{0,1:T(8,128)(2,1)}), (bf16[256,64]{0,1:T(8,128)(2,1)}, bf16[256,64]{0,1:T(8,128)(2,1)})) %all-reduce.20.cloned.1.call-update) | async-done | bytes 65552 | tf_op jit(solution)/shard_map/psum | solution.py:104
  136.3 81.2 %all-reduce.22.cloned.1.call-done = (bf16[256,512]{1,0:T(8,128)(2,1)}, bf16[256,512]{1,0:T(8,128)(2,1)}) async-done(((bf16[256,512]{1,0:T(8,128)(2,1)}, bf16[256,512]{1,0:T(8,128)(2,1)}), (bf16[256,512]{1,0:T(8,128)(2,1)}, bf16[256,512]{1,0:T(8,128)(2,1)})) %all-reduce.22.cloned.1.call-update) | async-done | bytes 524304 | tf_op jit(solution)/shard_map/psum | solution.py:102
  217.5 1.3 fusion
  219.9 1.6 fusion.11
  222.6 245.9 %all-reduce.3 = (bf16[256,64]{1,0:T(8,128)(2,1)S(1)}, f32[16]{0:T(128)S(1)}, f32[16]{0:T(128)S(1)}) all-reduce(f32[256,64]{1,0:T(8,128)S(1)} %fusion.22, f32[16]{0:T(128)S(1)} %get-tuple-element.9, f32[16]{0:T(128)S(1)} %get-tuple-element.8), channel_id=1, replica_groups=mesh['wide'=64,'narrow'=8] {'wide'}, use_global_device_ids=true, to_apply=%region_8.0 | all-reduce | flops 16416 | bytes 98560 | tf_op jit(solution)/shard_map/psum | solution.py:117
  470.1 1.0 multiply_reduce_fusion
  471.2 1.0 convolution_multiply_fusion.2
  472.2 45.1 %all-gather.2 = bf16[64,4,64]{2,1,0:T(4,128)(2,1)} all-gather(bf16[1,4,64]{2,1,0:T(4,128)(2,1)S(1)} %fusion.4), channel_id=1, replica_groups=mesh['wide'=64,'narrow'=8] {'wide'}, dimensions={0}, use_global_device_ids=true | all-gather | bytes 33280 | tf_op jit(solution)/shard_map/all_gather | solution.py:142
  517.3 52.5 %all-gather.1 = bf16[64,4,1024]{2,1,0:T(4,128)(2,1)} all-gather(bf16[1,4,1024]{2,1,0:T(4,128)(2,1)S(1)} %bitcast.54), channel_id=1, replica_groups=mesh['wide'=64,'narrow'=8] {'wide'}, dimensions={0}, use_global_device_ids=true | all-gather | bytes 532480 | tf_op jit(solution)/shard_map/all_gather | solution.py:140
  569.8 1.2 reshape.25
  571.0 1.2 convolution_convert_fusion
  572.3 12.8 %psum.102 = f32[4]{0:T(128)S(1)} all-reduce(f32[4]{0:T(128)S(1)} %broadcast_multiply_fusion.1), channel_id=1, replica_groups=mesh['wide'=64,'narrow'=8] {'narrow'}, use_global_device_ids=true, to_apply=%region_18.0 | all-reduce | flops 4 | bytes 32 | tf_op jit(solution)/shard_map/psum | solution.py:128
  585.6 22.4 %psum.99 = bf16[256,64]{1,0:T(8,128)(2,1)} all-reduce(bf16[256,64]{1,0:T(8,128)(2,1)} %bitcast.53), channel_id=1, replica_groups=mesh['wide'=64,'narrow'=8] {'narrow'}, use_global_device_ids=true, to_apply=%region_13.0 | all-reduce | flops 16384 | bytes 65536 | tf_op jit(solution)/shard_map/psum | solution.py:145
  608.1 1.7 fusion.24
  609.8 32.4 %all-reduce.14.cloned.1.call-done = bf16[256,512]{1,0:T(8,128)(2,1)} async-done(((bf16[256,512]{1,0:T(8,128)(2,1)}), bf16[256,512]{1,0:T(8,128)(2,1)}) %all-reduce.14.cloned.1.call-update) | async-done | bytes 262160 | tf_op jit(solution)/shard_map/psum | solution.py:144
  642.1 1.5 multiply_convert_fusion
  645.8 1.5 convolution_add_fusion
  647.3 246.0 %all-reduce.23 = (bf16[256,64]{0,1:T(8,128)(2,1)S(1)}, bf16[256,64]{0,1:T(8,128)(2,1)S(1)}) all-reduce(f32[256,64]{0,1:T(8,128)S(1)} %convolution_multiply_fusion.6, f32[256,64]{0,1:T(8,128)S(1)} %convolution_multiply_fusion.5), channel_id=1, replica_groups=mesh['wide'=64,'narrow'=8] {'wide'}, use_global_device_ids=true, to_apply=%region_15.0 | all-reduce | flops 32768 | bytes 196608 | tf_op jit(solution)/shard_map/psum | solution.py:159
  895.9 1.0 convolution_add_fusion.3
  897.8 1.7 copy.34
  (85 shorter events, 12.9 us)
Async XLA Ops:
  7.2 212.7 %copy-start = (bf16[512,1024]{1,0:T(8,128)(2,1)S(1)}, bf16[512,1024]{1,0:T(8,128)(2,1)}, u32[]{:S(2)}) copy-start(bf16[512,1024]{1,0:T(8,128)(2,1)} %param.21) | copy-start | bytes 3145732
  7.2 129.1 %all-reduce.20.cloned.1.call-start = ((), (), s32[]{:S(2)}) async-start(), calls=%async_computation.3 | async-start | bytes 131072 | tf_op jit(solution)/shard_map/psum | solution.py:104
  7.2 54.6 %copy-start.6 = (bf16[1024,64]{0,1:T(8,128)(2,1)S(1)}, bf16[1024,64]{0,1:T(8,128)(2,1)}, u32[]{:S(2)}) copy-start(bf16[1024,64]{0,1:T(8,128)(2,1)} %param.22) | copy-start | bytes 393220
  61.7 2.1 copy-start.1
  61.9 1.0 copy-start.7
  63.8 153.7 %all-reduce.22.cloned.1.call-start = ((), (), s32[]{:S(2)}) async-start(), calls=%async_computation.4 | async-start | bytes 1048576 | tf_op jit(solution)/shard_map/psum | solution.py:102
  63.9 1.2 copy-start.2
  66.2 151.2 %copy-start.10 = (bf16[64,512]{1,0:T(8,128)(2,1)S(1)}, bf16[64,512]{1,0:T(8,128)(2,1)}, u32[]{:S(2)}) copy-start(bf16[64,512]{1,0:T(8,128)(2,1)} %param.24) | copy-start | bytes 196612
  66.3 403.8 %all-reduce.16.cloned.1.call-start = ((), (), s32[]{:S(2)}) async-start(), calls=%async_computation.1 | async-start | bytes 2097152
  217.5 1.3 copy-start.15
  217.5 1.3 copy-start.17
  217.5 1.3 copy-start.20
  218.8 1.1 copy-start.9
  221.5 420.6 %all-reduce.14.cloned.1.call-start = ((), (), s32[]{:S(2)}) async-start(), calls=%async_computation | async-start | bytes 524288 | tf_op jit(solution)/shard_map/psum | solution.py:144
  222.6 247.5 %copy-start.13 = (bf16[64,1024]{1,0:T(8,128)(2,1)S(1)}, bf16[64,1024]{1,0:T(8,128)(2,1)}, u32[]{:S(2)}) copy-start(bf16[64,1024]{1,0:T(8,128)(2,1)} %param.27) | copy-start | bytes 393220
  469.1 0.9 copy-start.21
  572.2 69.9 %copy-start.5 = (f32[256,512]{1,0:T(8,128)S(1)}, f32[256,512]{1,0:T(8,128)}, u32[]{:S(2)}) copy-start(f32[256,512]{1,0:T(8,128)} %copy-done.4) | copy-start | bytes 1572868
  572.2 323.7 %all-reduce.18.cloned.1.call-start = ((), (), s32[]{:S(2)}) async-start(), calls=%async_computation.2 | async-start | bytes 2621440
  643.7 0.8 copy-start.11
  643.7 1.0 copy-start.12
  643.7 1.9 copy-start.16
  644.5 1.2 copy-start.3
  647.3 246.0 %copy-start.18 = (bf16[256,64]{0,1:T(8,128)(2,1)S(1)}, bf16[256,64]{0,1:T(8,128)(2,1)}, u32[]{:S(2)}) copy-start(bf16[256,64]{0,1:T(8,128)(2,1)} %get-tuple-element.18) | copy-start | bytes 98308
  895.9 1.1 copy-start.8
  (6 other events, 4.4 us)
Sparse Core Ops, SparseCore 0:
  63.9 72.3 all-reduce.19
  139.3 78.0 all-reduce.21
  221.7 198.1 all-reduce.15
  572.4 69.7 all-reduce.13
  647.4 200.1 all-reduce.17
where the time goes:
time: 911 us; the launch traced here: 906 us
  blocking collectives  679 us (75%)
  waiting for transfers between devices  180 us (20%)
  matrix products  21.7 us (2%)
  between operations  15.5 us (2%)
    psum x1, blocking collectives, shards(): lax.psum((gate_adapter_slice, up_adapter_slice), 'wide')  246 us
    psum x1, blocking collectives, shards(): lax.psum(frozen_product_rows(hidden_policy, a_down), 'wide')  246 us
    psum x1, waiting for transfers between devices, shards(): lax.psum(gate_part.astype(jnp.bfloat16), 'narrow').astype(jnp.float32)  81.2 us
    psum x1, waiting for transfers between devices, shards(): lax.psum(factor_gate_part.astype(jnp.bfloat16), 'narrow')  66.6 us
    all_gather x1, blocking collectives, shards(): gathered = lax.all_gather(tokens, 'wide', axis=0, tiled=True)  54.5 us
    all_gather x1, blocking collectives, shards(): lax.all_gather(output_gradient_rows, 'wide', axis=0, tiled=True)  52.5 us
    all_gather x1, blocking collectives, shards(): lax.all_gather(adapter_gradient_slice, 'wide', axis=0, tiled=True)  45.1 us
    psum x1, waiting for transfers between devices, shards(): lax.psum(hidden_part.astype(jnp.bfloat16), 'narrow').astype(jnp.float32)  32.4 us
  transfers between devices with their start and end apart: 5, of which 3 were waited for; matrix products, arithmetic and copies ran while one was open for 1% of the time, Pallas kernels for 0%

commit v1 on v0

v1 whole, which is shorter than its diff:
```python
import functools

import jax
import jax.numpy as jnp
from jax import lax
from jax.experimental import pallas as pl
from jax.experimental.pallas import tpu as pltpu
from jax.sharding import PartitionSpec as P

MESH = pl.DeviceIdType.MESH
BF16 = jnp.bfloat16
F32 = jnp.float32
D = 8192
TOKENS = 256
RANK = 64
ADAPTER_SCALE = 2.0
KL_WEIGHT = 0.1
NQ = 8
LANES = 128


def mm(a, b):
    return jnp.dot(a, b, preferred_element_type=F32)


def mm_nt(a, b):
    return lax.dot_general(a, b, (((1,), (1,)), ((), ())), preferred_element_type=F32)


def mm_tn(a, b):
    return lax.dot_general(a, b, (((0,), (0,)), ((), ())), preferred_element_type=F32)


class Plan:
    def __init__(self, wide, narrow, db, fb):
        self.nc = 2
        self.nx = 4 if wide == 64 else 2
        self.ny = wide // (self.nx * self.nc)
        self.nz = narrow
        self.wide = wide
        self.db, self.fb = db, fb
        self.th = 2 * wide
        self.tz = self.th // narrow
        self.bs = min(16, wide)
        self.yb = self.bs // (self.nx * 2)
        self.names, self.shapes = [], []
        nx, ny, nz, th, tz = self.nx, self.ny, self.nz, self.th, self.tz
        zw = 2 * fb + LANES
        v = self.vmem
        v("wgu", (db, 2 * fb), BF16)
        v("down", (fb, db), BF16)
        v("ag", (db, RANK), BF16)
        v("au", (db, RANK), BF16)
        v("agu", (db, LANES), BF16)
        v("bd", (LANES, 2 * fb), BF16)
        v("adown", (fb, RANK), BF16)
        v("bdown", (RANK, db), BF16)
        v("tok", (4, db), BF16)
        v("cot", (4, db), BF16)
        v("t32", (2, 16, LANES), F32)
        v("c32", (2, 16, LANES), F32)
        v("o32", (4, db), F32)
        self.dma("load", 10)
        for h in range(2):
            k = str(h)
            for g in "AD":
                v(g + "g" + k, (ny, nx, 2, 16, LANES), BF16)
                self.rem(g + "y" + k, ny - 1)
                self.rem(g + "x" + k, nx - 1)
                self.rem(g + "c" + k, 1)
            for g in "CF":
                v(g + "r" + k, (ny, nx, 2, 16, LANES), BF16)
                v(g + "rc" + k, (ny, nx, 16, LANES), BF16)
                v(g + "s1" + k, (ny, nx, 16, LANES), BF16)
                v(g + "rx" + k, (nx - 1, ny, 16, LANES), BF16)
                v(g + "s2" + k, (ny, 16, LANES), BF16)
                v(g + "ry" + k, (ny - 1, 16, LANES), BF16)
                self.rem(g + "c" + k, 1)
                self.rem(g + "x" + k, nx - 1)
                self.rem(g + "y" + k, ny - 1)
            for g, width in (("B", zw), ("E", fb)):
                v(g + "b" + k, (nz, tz, width), BF16)
                v(g + "r" + k, (nz - 1, tz, width), BF16)
                v(g + "g" + k, (nz, tz, width), BF16)
                self.rem(g + "rs" + k, nz - 1)
                self.rem(g + "ag" + k, nz - 1)
            v("x" + k, (th, db), BF16)
            v("go" + k, (th, db), BF16)
            v("hp" + k, (th, fb), BF16)
            v("su" + k, (th, 2 * fb), F32)
            v("ggu" + k, (th, 2 * fb), BF16)
        for g, rows in (("fd", th), ("ad", 2 * th)):
            part = rows // 2 // nx
            v(g + "p", (2, nx, part, LANES), BF16)
            v(g + "rc", (nx, part, LANES), BF16)
            v(g + "s1", (nx, part, LANES), BF16)
            v(g + "rx", (nx - 1, part, LANES), BF16)
            v(g + "s2", (part, LANES), BF16)
            v(g + "ry", (ny - 1, part, LANES), BF16)
            v(g + "f", (2, nx, part, LANES), BF16)
            self.rem(g + "c", 1)
            self.rem(g + "x", nx - 1)
            self.rem(g + "y", ny - 1)
            self.rem(g + "X", nx - 1)
            self.rem(g + "C", 1)
        v("gfb", (nz, tz, LANES), BF16)
        v("gfr", (nz - 1, tz, LANES), BF16)
        v("gfg", (nz, tz, LANES), BF16)
        self.rem("gfrs", nz - 1)
        self.rem("gfag", nz - 1)
        for name in ("st0", "st1", "st2", "stc", "dv"):
            v(name, (8, LANES), F32)
        v("stx", (nx - 1, 8, LANES), F32)
        v("sty", (ny - 1, 8, LANES), F32)
        v("dvr", (nz - 1, 8, LANES), F32)
        self.rem("stc_", 1)
        self.rem("stx_", nx - 1)
        self.rem("sty_", ny - 1)
        self.rem("dv_", nz - 1)

    def vmem(self, name, shape, dtype):
        self.names.append(name)
        self.shapes.append(pltpu.VMEM(shape, dtype))

    def dma(self, name, count):
        self.names.append(name)
        self.shapes.append(pltpu.SemaphoreType.DMA((count,)))

    def rem(self, name, count):
        self.dma(name + ">", count)
        self.dma(name + "<", count)


def step_kernel(plan, *refs):
    (tokens, cotangent, rewards, group_ids, token_mask, w_gate, w_up, down_w, a_gate, a_up,
     gate_of, up_of, a_down, down_of) = refs[:14]
    (gx_o, dv_o, ad_o, x_o, gu_o, gad_o, dog_o) = refs[14:21]
    r = dict(zip(plan.names, refs[21:]))
    ny, nx, nz, th, tz, db, fb = plan.ny, plan.nx, plan.nz, plan.th, plan.tz, plan.db, plan.fb
    w = lax.axis_index("wide")
    z = lax.axis_index("narrow")
    y, x, c = w // (nx * 2), (w // 2) % nx, w % 2
    other = 1 - c

    def wide_of(yy, xx, cc):
        return (yy * nx + xx) * 2 + cc

    ys = [(y + d) % ny for d in range(1, ny)]
    xs = [(x + d) % nx for d in range(1, nx)]
    zs = [(z + d) % nz for d in range(1, nz)]
    dev_y = [(wide_of(v, x, c), z) for v in ys]
    dev_x = [(wide_of(y, v, c), z) for v in xs]
    dev_c = (wide_of(y, x, other), z)
    dev_z = [(w, v) for v in zs]
    peers = dev_y + dev_x + [dev_c] + dev_z

    barrier = pltpu.get_barrier_semaphore()
    for peer in peers:
        pl.semaphore_signal(barrier, inc=1, device_id=peer, device_id_type=MESH)

    loads = []
    for src, dst in (
        (tokens, r["tok"]), (w_gate, r["wgu"].at[:, :fb]), (w_up, r["wgu"].at[:, fb:]),
        (a_gate, r["ag"]), (a_up, r["au"]), (gate_of, r["bd"].at[:RANK, :fb]),
        (up_of, r["bd"].at[RANK:, fb:]), (cotangent, r["cot"]), (down_w, r["down"]),
        (a_down, r["adown"]),
    ):
        copy = pltpu.make_async_copy(src, dst, r["load"].at[len(loads)])
        copy.start()
        loads.append(copy)

    pending = []
    flying = {}

    def send(name, index, src, dst, device):
        copy = pltpu.make_async_remote_copy(
            src_ref=src, dst_ref=dst, send_sem=r[name + ">"].at[index],
            recv_sem=r[name + "<"].at[index], device_id=device, device_id_type=MESH,
        )
        copy.start()
        pending.append(copy)
        flying.setdefault(name, []).append(copy)

    def arrive(name):
        for copy in flying.pop(name):
            copy.wait_recv()

    def gather_y(g, k):
        buf = r[g + "g" + k]
        for i, device in enumerate(dev_y):
            send(g + "y" + k, i, buf.at[y, x, c], buf.at[y, x, c], device)

    def gather_x(g, k):
        buf = r[g + "g" + k]
        arrive(g + "y" + k)
        for i, device in enumerate(dev_x):
            send(g + "x" + k, i, buf.at[:, x, c], buf.at[:, x, c], device)

    def gather_c(g, k):
        buf = r[g + "g" + k]
        arrive(g + "x" + k)
        send(g + "c" + k, 0, buf.at[:, :, c], buf.at[:, :, c], dev_c)

    def scatter_c(g, k):
        buf = r[g + "r" + k]
        send(g + "c" + k, 0, buf.at[:, :, other], r[g + "rc" + k], dev_c)

    def scatter_x(g, k):
        arrive(g + "c" + k)
        total = r[g + "r" + k][:, :, c].astype(F32) + r[g + "rc" + k][...].astype(F32)
        r[g + "s1" + k][...] = total.astype(BF16)
        for i, device in enumerate(dev_x):
            send(g + "x" + k, i, r[g + "s1" + k].at[:, xs[i]], r[g + "rx" + k].at[i], device)

    def scatter_y(g, k):
        arrive(g + "x" + k)
        total = r[g + "s1" + k][:, x].astype(F32)
        for i in range(nx - 1):
            total += r[g + "rx" + k][i].astype(F32)
        r[g + "s2" + k][...] = total.astype(BF16)
        for i, device in enumerate(dev_y):
            send(g + "y" + k, i, r[g + "s2" + k].at[ys[i]], r[g + "ry" + k].at[i], device)

    def scatter_end(g, k):
        arrive(g + "y" + k)
        total = r[g + "s2" + k][y].astype(F32)
        for i in range(ny - 1):
            total += r[g + "ry" + k][i].astype(F32)
        return total

    def narrow_sum(b, g, k):
        for i, device in enumerate(dev_z):
            send(g + "rs" + k, i, r[b + k].at[zs[i]], r[g + "r" + k].at[i], device)

    def narrow_hand(b, g, k):
        arrive(g + "rs" + k)
        total = r[b + k][z].astype(F32)
        for i in range(nz - 1):
            total += r[g + "r" + k][i].astype(F32)
        r[g + "g" + k][z] = total.astype(BF16)
        for i, device in enumerate(dev_z):
            send(g + "ag" + k, i, r[g + "g" + k].at[z], r[g + "g" + k].at[z], device)

    def small_c(g):
        send(g + "c", 0, r[g + "p"].at[other], r[g + "rc"], dev_c)

    def small_x(g):
        arrive(g + "c")
        r[g + "s1"][...] = (r[g + "p"][c].astype(F32) + r[g + "rc"][...].astype(F32)).astype(BF16)
        for i, device in enumerate(dev_x):
            send(g + "x", i, r[g + "s1"].at[xs[i]], r[g + "rx"].at[i], device)

    def small_y(g):
        arrive(g + "x")
        total = r[g + "s1"][x].astype(F32)
        for i in range(nx - 1):
            total += r[g + "rx"][i].astype(F32)
        r[g + "s2"][...] = total.astype(BF16)
        for i, device in enumerate(dev_y):
            send(g + "y", i, r[g + "s2"], r[g + "ry"].at[i], device)

    def small_X(g):
        arrive(g + "y")
        total = r[g + "s2"][...].astype(F32)
        for i in range(ny - 1):
            total += r[g + "ry"][i].astype(F32)
        r[g + "f"][c, x] = total.astype(BF16)
        for i, device in enumerate(dev_x):
            send(g + "X", i, r[g + "f"].at[c, x], r[g + "f"].at[c, x], device)

    def small_C(g):
        arrive(g + "X")
        send(g + "C", 0, r[g + "f"].at[c], r[g + "f"].at[c], dev_c)

    rows = plan.bs * 16
    row = lax.broadcasted_iota(jnp.int32, (rows, rows), 0)
    col = lax.broadcasted_iota(jnp.int32, (rows, rows), 1)

    def by_block(v):
        return ((v >> 1) & 7) * (2 * plan.bs) + (v >> 4) * 2 + (v & 1)

    to_tokens = (row == by_block(col)).astype(F32).astype(BF16)
    to_shards = (col == by_block(row)).astype(F32).astype(BF16)

    def unpack(g, k, out):
        for b in range(plan.wide // plan.bs):
            block = r[g + "g" + k][plan.yb * b:plan.yb * (b + 1)].reshape(rows, LANES)
            turned = mm(to_tokens, block).astype(BF16)
            n = 2 * plan.bs
            for q in range(NQ):
                out[n * b:n * (b + 1), LANES * q:LANES * (q + 1)] = turned[n * q:n * (q + 1)]

    def pack(value, g, k):
        for b in range(plan.wide // plan.bs):
            n = 2 * plan.bs
            block = jnp.concatenate(
                [value[n * b:n * (b + 1), LANES * q:LANES * (q + 1)] for q in range(NQ)], axis=0)
            turned = mm(to_shards, block).astype(BF16)
            r[g + "r" + k][plan.yb * b:plan.yb * (b + 1)] = turned.reshape(
                plan.yb, nx, 2, 16, LANES)

    loads[0].wait()
    tok = r["tok"][...].astype(F32)
    for h in range(2):
        for q in range(NQ):
            r["t32"][h, 2 * q:2 * q + 2, :] = tok[2 * h:2 * h + 2, LANES * q:LANES * (q + 1)]
        r["Ag" + str(h)][y, x, c] = r["t32"][h].astype(BF16)

    pl.semaphore_wait(barrier, len(peers))
    gather_y("A", "0")
    gather_y("A", "1")

    lane = lax.broadcasted_iota(jnp.int32, (1, LANES), 1)
    mask = [token_mask[t].astype(F32) for t in range(4)]
    reward = [rewards[t] for t in range(4)]
    ids = [group_ids[t] for t in range(4)]
    reward_row = jnp.zeros((1, LANES), F32)
    count_row = jnp.zeros((1, LANES), F32)
    for t in range(4):
        reward_row += jnp.where(lane == ids[t], mask[t] * reward[t], 0.0)
        count_row += jnp.where(lane == ids[t], mask[t], 0.0)
    row8 = lax.broadcasted_iota(jnp.int32, (8, LANES), 0)
    r["st0"][...] = jnp.where(row8 == 0, reward_row, jnp.where(row8 == 1, count_row, 0.0))
    send("stc_", 0, r["st0"], r["stc"], dev_c)

    loads[7].wait()
    cot = r["cot"][...].astype(F32)
    for h in range(2):
        for q in range(NQ):
            r["c32"][h, 2 * q:2 * q + 2, :] = cot[2 * h:2 * h + 2, LANES * q:LANES * (q + 1)]
    for i in (3, 4, 5, 6):
        loads[i].wait()
    r["agu"][:, :RANK] = r["ag"][...]
    r["agu"][:, RANK:] = r["au"][...]
    r["bd"][:RANK, fb:] = jnp.zeros((RANK, fb), BF16)
    r["bd"][RANK:, :fb] = jnp.zeros((RANK, fb), BF16)
    bdown_load = pltpu.make_async_copy(down_of, r["bdown"], r["load"].at[0])
    bdown_load.start()

    arrive("stc_")
    r["st1"][...] = r["st0"][...] + r["stc"][...]
    for i, device in enumerate(dev_x):
        send("stx_", i, r["st1"], r["stx"].at[i], device)

    gather_x("A", "0")
    gather_x("A", "1")

    arrive("stx_")
    total = r["st1"][...]
    for i in range(nx - 1):
        total += r["stx"][i]
    r["st2"][...] = total
    for i, device in enumerate(dev_y):
        send("sty_", i, r["st2"], r["sty"].at[i], device)

    gather_c("A", "0")
    gather_c("A", "1")
    loads[1].wait()
    loads[2].wait()

    for h in range(2):
        k = str(h)
        arrive("Ac" + k)
        unpack("A", k, r["x" + k])
        xv = r["x" + k][...]
        r["Bb" + k][:, :, 2 * fb:] = mm(xv, r["agu"][...]).astype(BF16).reshape(nz, tz, LANES)
        r["Bb" + k][:, :, :2 * fb] = mm(xv, r["wgu"][...]).astype(BF16).reshape(nz, tz, 2 * fb)
        narrow_sum("Bb", "B", k)

    arrive("sty_")
    stats = r["st2"][...]
    for i in range(ny - 1):
        stats += r["sty"][i]
    group_count = stats[1:2]
    group_mean = stats[0:1] / jnp.maximum(group_count, 1.0)
    all_count = jnp.sum(group_count, axis=1, keepdims=True)
    scale_of = TOKENS / jnp.maximum(all_count, 1.0)
    advantage, token_scale = [], []
    for t in range(4):
        mean_t = jnp.sum(jnp.where(lane == ids[t], group_mean, 0.0), axis=1, keepdims=True)
        advantage.append(reward[t] - mean_t)
        token_scale.append(mask[t] * scale_of)

    narrow_hand("Bb", "B", "0")
    narrow_hand("Bb", "B", "1")
    loads[8].wait()
    loads[9].wait()
    bdown_load.wait()

    fd_parts = []
    for h in range(2):
        k = str(h)
        arrive("Bag" + k)
        both = r["Bg" + k][...].reshape(th, 2 * fb + LANES)
        adapt = ADAPTER_SCALE * mm(both[:, 2 * fb:], r["bd"][...])
        gate_base = both[:, :fb].astype(F32)
        up_base = both[:, fb:2 * fb].astype(F32)
        gate = gate_base + adapt[:, :fb]
        up = up_base + adapt[:, fb:]
        sig = jax.nn.sigmoid(gate)
        silu = gate * sig
        slope = sig * (1.0 + gate * (1.0 - sig))
        full = silu * up
        hp = full.astype(BF16)
        hd = (full - gate_base * jax.nn.sigmoid(gate_base) * up_base).astype(BF16)
        r["hp" + k][...] = hp
        r["su" + k][:, :fb] = up * slope
        r["su" + k][:, fb:] = silu
        fd = mm(hp, r["adown"][...])
        fd_parts.append(fd)
        out = mm(hd, r["down"][...]) + ADAPTER_SCALE * mm(fd.astype(BF16), r["bdown"][...])
        pack(out.astype(BF16), "C", k)
        scatter_c("C", k)
    fd_both = jnp.concatenate(fd_parts, axis=1).astype(BF16)
    r["fdp"][...] = fd_both.reshape(2, nx, th // 2 // nx, LANES)
    small_c("fd")

    scatter_x("C", "0")
    scatter_x("C", "1")
    small_x("fd")
    scatter_y("C", "0")
    scatter_y("C", "1")
    small_y("fd")

    row16 = lax.broadcasted_iota(jnp.int32, (16, 1), 0)
    even = (row16 & 1) == 0
    div = []
    for h in range(2):
        k = str(h)
        od = scatter_end("C", k)
        square = od * od
        for t in range(2):
            picked = jnp.where(((row16 & 1) == t), square, 0.0)
            div.append(jnp.sum(jnp.sum(picked, axis=1, keepdims=True), axis=0, keepdims=True))
        adv = jnp.where(even, advantage[2 * h], advantage[2 * h + 1])
        scl = jnp.where(even, token_scale[2 * h], token_scale[2 * h + 1])
        grad = scl * (KL_WEIGHT * od - adv * r["c32"][h])
        r["Dg" + k][y, x, c] = grad.astype(BF16)
        gather_y("D", k)
    dv = jnp.zeros((8, LANES), F32)
    for t in range(4):
        dv += jnp.where(row8 == t, div[t], 0.0)
    r["dv"][...] = dv * (0.5 / D)
    for i, device in enumerate(dev_z):
        send("dv_", i, r["dv"], r["dvr"].at[i], device)
    small_X("fd")
    gather_x("D", "0")
    gather_x("D", "1")
    small_C("fd")
    gather_c("D", "0")
    gather_c("D", "1")

    gf_parts = []
    for h in range(2):
        k = str(h)
        arrive("Dc" + k)
        unpack("D", k, r["go" + k])
        go = r["go" + k][...]
        gf = ADAPTER_SCALE * mm_nt(go, r["bdown"][...])
        gf_parts.append(gf)
        gh = mm_nt(go, r["down"][...]) + mm_nt(gf.astype(BF16), r["adown"][...])
        r["Eb" + k][...] = gh.astype(BF16).reshape(nz, tz, fb)
        narrow_sum("Eb", "E", k)
    gf_both = jnp.concatenate(gf_parts, axis=1).astype(BF16)
    r["gfb"][...] = gf_both.reshape(nz, tz, LANES)
    for i, device in enumerate(dev_z):
        send("gfrs", i, r["gfb"].at[zs[i]], r["gfr"].at[i], device)

    narrow_hand("Eb", "E", "0")
    narrow_hand("Eb", "E", "1")
    arrive("gfrs")
    total = r["gfb"][z].astype(F32)
    for i in range(nz - 1):
        total += r["gfr"][i].astype(F32)
    r["gfg"][z] = total.astype(BF16)
    for i, device in enumerate(dev_z):
        send("gfag", i, r["gfg"].at[z], r["gfg"].at[z], device)

    half = th // 2 // nx * 2
    for h in range(2):
        k = str(h)
        arrive("Eag" + k)
        gh = r["Eg" + k][...].reshape(th, fb).astype(F32)
        r["ggu" + k][:, :fb] = (gh * r["su" + k][:, :fb]).astype(BF16)
        r["ggu" + k][:, fb:] = (gh * r["su" + k][:, fb:]).astype(BF16)
        ggu = r["ggu" + k][...]
        ad = (ADAPTER_SCALE * mm_nt(ggu, r["bd"][...])).astype(BF16)
        r["adp"][h] = ad.reshape(nx, half, LANES)
        gx = mm_nt(ggu, r["wgu"][...]) + mm_nt(ad, r["agu"][...])
        pack(gx.astype(BF16), "F", k)
        scatter_c("F", k)
    small_c("ad")

    scatter_x("F", "0")
    scatter_x("F", "1")
    small_x("ad")
    gu = jnp.zeros((LANES, 2 * fb), F32)
    for h in range(2):
        k = str(h)
        factors = r["Bg" + k][:, :, 2 * fb:].reshape(th, LANES)
        gu += mm_tn(factors, r["ggu" + k][...])
    gu_o[...] = ADAPTER_SCALE * gu
    scatter_y("F", "0")
    scatter_y("F", "1")
    small_y("ad")

    arrive("fdC")
    fdf = r["fdf"][...].reshape(th, LANES)
    dog = mm_tn(fdf, r["go0"][...])[:RANK] + mm_tn(fdf, r["go1"][...])[RANK:]
    dog_o[...] = ADAPTER_SCALE * dog
    arrive("gfag")
    gff = r["gfg"][...].reshape(th, LANES)
    gad_o[...] = mm_tn(r["hp0"][...], gff)[:, :RANK] + mm_tn(r["hp1"][...], gff)[:, RANK:]
    arrive("dv_")
    total = r["dv"][...]
    for i in range(nz - 1):
        total += r["dvr"][i]
    dv_o[...] = total
    small_X("ad")
    for h in range(2):
        k = str(h)
        gx = scatter_end("F", k)
        for q in range(NQ):
            r["o32"][2 * h:2 * h + 2, LANES * q:LANES * (q + 1)] = gx[2 * q:2 * q + 2]
    gx_o[...] = r["o32"][...].astype(BF16)
    small_C("ad")
    for h in range(2):
        x_o[h * th:(h + 1) * th] = r["x" + str(h)][...]
    arrive("adC")
    ad_o[...] = r["adf"][...].reshape(2 * th, LANES)

    for copy in pending:
        copy.wait_send()


def finish_kernel(fb, gx, dv, ad, xv, gu, gad, dog, gx_o, dv_o, ag_o, au_o, gog_o, uog_o, gad_o,
                  dog_o):
    both = mm_tn(xv[...], ad[...])
    ag_o[...] = both[:, :RANK]
    au_o[...] = both[:, RANK:]
    gx_o[...] = gx[...]
    for t in range(4):
        dv_o[t] = jnp.max(dv[t:t + 1, :])
    gog_o[...] = gu[:RANK, :fb]
    uog_o[...] = gu[RANK:, fb:]
    gad_o[...] = gad[...]
    dog_o[...] = dog[...]


def shards(wide, narrow, tokens, cotangent, rewards, group_ids, token_mask, w_gate, w_up, down_w,
           a_gate, a_up, gate_of, up_of, a_down, down_of):
    db, fb = w_gate.shape
    plan = Plan(wide, narrow, db, fb)
    anyspace = pl.BlockSpec(memory_space=pl.ANY)
    vm = pl.BlockSpec(memory_space=pltpu.VMEM)
    sm = pl.BlockSpec(memory_space=pltpu.SMEM)
    s = jax.ShapeDtypeStruct
    mids = pl.pallas_call(
        functools.partial(step_kernel, plan),
        out_shape=(
            s((4, db), BF16), s((8, LANES), F32), s((2 * plan.th, LANES), BF16),
            s((2 * plan.th, db), BF16), s((LANES, 2 * fb), F32), s((fb, RANK), F32),
            s((RANK, db), F32),
        ),
        in_specs=[anyspace, anyspace, sm, sm, sm] + [anyspace] * 9,
        out_specs=(vm,) * 7,
        scratch_shapes=plan.shapes,
        compiler_params=pltpu.CompilerParams(
            collective_id=0, has_side_effects=True, vmem_limit_bytes=48 << 20),
        name="policy_step",
    )(tokens, cotangent, rewards, group_ids, token_mask, w_gate, w_up, down_w, a_gate, a_up,
      gate_of, up_of, a_down, down_of)
    outs = pl.pallas_call(
        functools.partial(finish_kernel, fb),
        out_shape=(
            s((4, db), BF16), s((4,), F32), s((db, RANK), F32), s((db, RANK), F32),
            s((RANK, fb), F32), s((RANK, fb), F32), s((fb, RANK), F32), s((RANK, db), F32),
        ),
        in_specs=[vm] * 7,
        out_specs=(vm, sm) + (vm,) * 6,
        compiler_params=pltpu.CompilerParams(vmem_limit_bytes=32 << 20),
        name="finish",
    )(*mids)
    return outs


def solution(mesh):
    return jax.shard_map(
        functools.partial(shards, mesh.shape["wide"], mesh.shape["narrow"]),
        mesh=mesh,
        in_specs=(
            P("wide", "narrow"),
            P("wide", "narrow"),
            P("wide"),
            P("wide"),
            P("wide"),
            P("narrow", "wide"),
            P("narrow", "wide"),
            P("wide", "narrow"),
            P("narrow", None),
            P("narrow", None),
            P(None, "wide"),
            P(None, "wide"),
            P("wide", None),
            P(None, "narrow"),
        ),
        out_specs=(
            P("wide", "narrow"),
            P("wide"),
            P("narrow", None),
            P("narrow", None),
            P(None, "wide"),
            P(None, "wide"),
            P("wide", None),
            P(None, "narrow"),
        ),
        check_vma=False,
    )
```

time: 911 us -> 126 us (0.14)
  blocking collectives: 679 us -> 0 us
  waiting for transfers between devices: 180 us -> 0 us
  Pallas kernels: 0 us -> 116 us
  matrix products: 21.7 us -> 0 us
  between operations: 15.5 us -> 0.75 us
    psum x4 -> x0, blocking collectives: 527 us -> none  [the longest x1 246 us: shards(): lax.psum((gate_adapter_slice, up_adapter_slice), 'wide')]
    psum x3 -> x0, waiting for transfers between devices: 180 us -> none  [the longest x1 81.2 us: shards(): lax.psum(gate_part.astype(jnp.bfloat16), 'narrow').astype(jnp.float32)]
    all_gather x3 -> x0, blocking collectives: 152 us -> none  [the longest x1 54.5 us: shards(): gathered = lax.all_gather(tokens, 'wide', axis=0, tiled=True)]
    pallas_call x0 -> x2, Pallas kernels: none -> 116 us  [the longest x1 115 us: shards(): pl.pallas_call(functools.partial(step_kernel, plan), out_shape=(s((4, db)...]
    dot_general x24 -> x0, matrix products: 21.7 us -> none  [the longest x9 8.51 us: frozen_product_rows(): return jnp.dot(operand, weights, preferred_element_type=jnp.float32)]
  transfers between devices with their start and end apart: 5 -> 0, of which waited for: 3 -> 0; matrix products, arithmetic and copies ran while one was open for 1% -> 0% of each run, Pallas kernels for 0% -> 0%
where the time goes in v1:
time: 126 us
  Pallas kernels  116 us (92%)
  local copies, waits for them, and re-layouts  9 us (7%)
    pallas_call x1, Pallas kernels, shards(): pl.pallas_call(functools.partial(step_kernel, plan), out_shape=(s((4, db)...  115 us
    unnamed x29, local copies, waits for them, and re-layouts  6.46 us
    pallas_call x3, local copies, waits for them, and re-layouts, shards(): pl.pallas_call(functools.partial(finish_kernel, fb), out_shape=(s((4, db)...  2.55 us

profile of v1, /device:TPU:1, one launch (start us, length us, event | category | flops | bytes accessed | tf_op | source)
XLA Modules:
  0.0 126.0 jit_solution(17989222947710755169)
XLA Ops:
  0.6 0.0 copy-start.11
  0.6 1.0 copy.24.refs_12_
  1.6 0.0 copy-done.11
  1.6 0.0 copy-start.12
  1.7 0.2 copy.22.refs_8_
  1.8 0.7 copy-done.12
  2.6 0.0 copy-start.7
  2.6 0.0 copy-start.8
  2.6 0.0 copy-start.9
  2.6 0.0 copy-start.10
  2.6 0.2 copy.23.refs_9_
  2.8 0.7 copy-done.3
  3.5 0.0 copy-done.4
  3.5 0.0 copy-done.5
  3.5 0.0 copy-done.8
  3.5 0.0 copy-start
  3.5 1.2 copy-done
  4.7 1.2 copy-done.1
  6.0 1.2 copy-done.2
  7.2 115.1 %policy_step.1 = (bf16[4,1024]{1,0:T(4,128)(2,1)S(1)}, f32[8,128]{1,0:T(8,128)S(1)}, bf16[256,128]{1,0:T(8,128)(2,1)S(1)}, bf16[256,1024]{1,0:T(8,128)(2,1)S(1)}...) custom-call(bf16[4,1024]{1,0:T(4,128)(2,1)S(1)} %copy-done.6, ...), custom_call_target="tpu_custom_call" | custom-call | tf_op jit(solution)/shard_map/policy_step/pallas_call | solution.py:558
  122.3 1.2 finish.1
  123.5 0.8 copy.27
  124.3 0.9 copy.25
  125.2 0.9 copy.26
  (10 shorter events, 0.0 us)
Async XLA Ops:
  0.6 1.0 copy-start.11
  1.6 0.9 copy-start.12
  2.6 0.9 copy-start.3
  2.6 0.9 copy-start.4
  2.6 0.9 copy-start.5
  2.6 0.9 copy-start.6
  2.6 0.9 copy-start.7
  2.6 0.9 copy-start.8
  2.6 0.9 copy-start.9
  2.6 0.9 copy-start.10
  3.5 1.2 copy-start
  4.7 1.2 copy-start.1
  6.0 1.2 copy-start.2

commit v2 on v1

v2 whole, which is shorter than its diff:
```python
import functools

import jax
import jax.numpy as jnp
from jax import lax
from jax.experimental import pallas as pl
from jax.experimental.pallas import tpu as pltpu
from jax.sharding import PartitionSpec as P

MESH = pl.DeviceIdType.MESH
BF16 = jnp.bfloat16
F32 = jnp.float32
D = 8192
TOKENS = 256
RANK = 64
ADAPTER_SCALE = 2.0
KL_WEIGHT = 0.1
NQ = 8
LANES = 128


def mm(a, b):
    return jnp.dot(a, b, preferred_element_type=F32)


def mm_nt(a, b):
    return lax.dot_general(a, b, (((1,), (1,)), ((), ())), preferred_element_type=F32)


def mm_tn(a, b):
    return lax.dot_general(a, b, (((0,), (0,)), ((), ())), preferred_element_type=F32)


class Plan:
    def __init__(self, wide, narrow, db, fb):
        self.nx = 4 if wide == 64 else 2
        self.ny = wide // (self.nx * 2)
        self.ne = 2 * self.nx
        self.nz = narrow
        self.wide = wide
        self.db, self.fb = db, fb
        self.th = 2 * wide
        self.tz = self.th // narrow
        self.bs = min(16, wide)
        self.yb = self.bs // self.ne
        self.names, self.shapes = [], []
        nx, ny, nz, ne, th, tz = self.nx, self.ny, self.nz, self.ne, self.th, self.tz
        v = self.vmem
        v("wgu", (db, 2 * fb), BF16)
        v("downx", (fb + LANES, db), BF16)
        v("agu", (LANES, db), BF16)
        v("bd", (LANES, 2 * fb), BF16)
        v("adown", (RANK, fb), BF16)
        v("tok", (4, db), BF16)
        v("cot", (4, db), BF16)
        v("t32", (2, 16, LANES), F32)
        v("c32", (2, 16, LANES), F32)
        v("o32", (4, db), F32)
        v("x", (2 * th, db), BF16)
        v("gx", (4, db), BF16)
        v("gab", (LANES, db), F32)
        v("gu", (LANES, 2 * fb), F32)
        v("gad", (RANK, fb), F32)
        v("dog", (RANK, db), F32)
        self.dma("load", 11)
        self.dma("out", 7)
        for h in range(2):
            k = str(h)
            for g in "AD":
                v(g + "g" + k, (ny, nx, 2, 16, LANES), BF16)
                self.rem(g + "y" + k, ny - 1)
                self.rem(g + "x" + k, nx - 1)
                self.rem(g + "c" + k, 1)
            for g in "CF":
                v(g + "r" + k, (ny, nx, 2, 16, LANES), BF16)
                v(g + "rc" + k, (ny, nx, 16, LANES), BF16)
                v(g + "s1" + k, (ny, nx, 16, LANES), BF16)
                v(g + "rx" + k, (nx - 1, ny, 16, LANES), BF16)
                v(g + "s2" + k, (ny, 16, LANES), BF16)
                v(g + "ry" + k, (ny - 1, 16, LANES), BF16)
                self.rem(g + "c" + k, 1)
                self.rem(g + "x" + k, nx - 1)
                self.rem(g + "y" + k, ny - 1)
            for g, width in (("B", 2 * fb + LANES), ("E", fb)):
                v(g + "b" + k, (nz, tz, width), BF16)
                v(g + "r" + k, (nz - 1, tz, width), BF16)
                self.rem(g + "rs" + k, nz - 1)
            for g, width in (("H", fb + LANES), ("K", 3 * fb + LANES), ("E", fb)):
                v(g + "g" + k, (nz, tz, width), BF16)
                self.rem(g + "ag" + k, nz - 1)
            v("go" + k, (th, db), BF16)
            v("ggu" + k, (th, 2 * fb), BF16)
        for g, rows in (("fd", th), ("ad", 2 * th)):
            part = rows // ne
            v(g + "p", (ne, part, LANES), BF16)
            v(g + "re", (ne - 1, part, LANES), BF16)
            v(g + "s", (part, LANES), BF16)
            v(g + "ry", (ny - 1, part, LANES), BF16)
            v(g + "f", (ne, part, LANES), BF16)
            self.rem(g + "e", ne - 1)
            self.rem(g + "y", ny - 1)
            self.rem(g + "E", ne - 1)
        v("Gb", (nz, tz, LANES), BF16)
        v("Gr", (nz - 1, tz, LANES), BF16)
        v("Gg", (nz, tz, LANES), BF16)
        self.rem("Grs", nz - 1)
        self.rem("Gag", nz - 1)
        for name in ("st0", "st1", "dv"):
            v(name, (8, LANES), F32)
        v("ste", (ne - 1, 8, LANES), F32)
        v("sty", (ny - 1, 8, LANES), F32)
        v("dvr", (nz - 1, 8, LANES), F32)
        self.rem("ste_", ne - 1)
        self.rem("sty_", ny - 1)
        self.rem("dv_", nz - 1)

    def vmem(self, name, shape, dtype):
        self.names.append(name)
        self.shapes.append(pltpu.VMEM(shape, dtype))

    def dma(self, name, count):
        self.names.append(name)
        self.shapes.append(pltpu.SemaphoreType.DMA((count,)))

    def rem(self, name, count):
        self.dma(name + ">", count)
        self.dma(name + "<", count)


def step_kernel(plan, *refs):
    (tokens, cotangent, rewards, group_ids, token_mask, w_gate, w_up, down_w, a_gate, a_up,
     gate_of, up_of, a_down, down_of) = refs[:14]
    (gx_o, dv_o, ag_o, au_o, gog_o, uog_o, gad_o, dog_o) = refs[14:22]
    r = dict(zip(plan.names, refs[22:]))
    ny, nx, nz, ne, th, tz, db, fb = (
        plan.ny, plan.nx, plan.nz, plan.ne, plan.th, plan.tz, plan.db, plan.fb)
    w = lax.axis_index("wide")
    z = lax.axis_index("narrow")
    y, x, c = w // ne, (w // 2) % nx, w % 2
    e = w % ne
    other = 1 - c

    ys = [(y + d) % ny for d in range(1, ny)]
    xs = [(x + d) % nx for d in range(1, nx)]
    es = [(e + d) % ne for d in range(1, ne)]
    zs = [(z + d) % nz for d in range(1, nz)]
    dev_y = [(v * ne + e, z) for v in ys]
    dev_x = [(y * ne + v * 2 + c, z) for v in xs]
    dev_e = [(y * ne + v, z) for v in es]
    dev_c = (y * ne + x * 2 + other, z)
    dev_z = [(w, v) for v in zs]
    peers = dev_y + dev_e + dev_z

    barrier = pltpu.get_barrier_semaphore()
    for peer in peers:
        pl.semaphore_signal(barrier, inc=1, device_id=peer, device_id_type=MESH)

    loads = []
    for src, dst in (
        (tokens, r["tok"]), (w_gate, r["wgu"].at[:, :fb]), (w_up, r["wgu"].at[:, fb:]),
        (a_gate, r["agu"].at[:RANK]), (a_up, r["agu"].at[RANK:]),
        (gate_of, r["bd"].at[:RANK, :fb]), (up_of, r["bd"].at[RANK:, fb:]),
        (cotangent, r["cot"]), (down_w, r["downx"].at[:fb]),
        (down_of, r["downx"].at[fb:fb + RANK]), (down_of, r["downx"].at[fb + RANK:]),
    ):
        copy = pltpu.make_async_copy(src, dst, r["load"].at[len(loads)])
        copy.start()
        loads.append(copy)

    pending = []
    flying = {}
    stores = []

    def store(src, dst):
        copy = pltpu.make_async_copy(src, dst, r["out"].at[len(stores)])
        copy.start()
        stores.append(copy)

    def send(name, index, src, dst, device):
        copy = pltpu.make_async_remote_copy(
            src_ref=src, dst_ref=dst, send_sem=r[name + ">"].at[index],
            recv_sem=r[name + "<"].at[index], device_id=device, device_id_type=MESH,
        )
        copy.start()
        pending.append(copy)
        flying.setdefault(name, []).append(copy)

    def arrive(name):
        for copy in flying.pop(name):
            copy.wait_recv()

    def add_up(total, slots, count):
        total = total.astype(F32)
        for i in range(count):
            total += slots[i].astype(F32)
        return total

    def gather_y(g, k):
        buf = r[g + "g" + k]
        for i, device in enumerate(dev_y):
            send(g + "y" + k, i, buf.at[y, x, c], buf.at[y, x, c], device)

    def gather_x(g, k):
        buf = r[g + "g" + k]
        arrive(g + "y" + k)
        for i, device in enumerate(dev_x):
            send(g + "x" + k, i, buf.at[:, x, c], buf.at[:, x, c], device)

    def gather_c(g, k):
        buf = r[g + "g" + k]
        arrive(g + "x" + k)
        send(g + "c" + k, 0, buf.at[:, :, c], buf.at[:, :, c], dev_c)

    def scatter_c(g, k):
        buf = r[g + "r" + k]
        send(g + "c" + k, 0, buf.at[:, :, other], r[g + "rc" + k], dev_c)

    def scatter_x(g, k):
        arrive(g + "c" + k)
        total = r[g + "r" + k][:, :, c].astype(F32) + r[g + "rc" + k][...].astype(F32)
        r[g + "s1" + k][...] = total.astype(BF16)
        for i, device in enumerate(dev_x):
            send(g + "x" + k, i, r[g + "s1" + k].at[:, xs[i]], r[g + "rx" + k].at[i], device)

    def scatter_y(g, k):
        arrive(g + "x" + k)
        total = add_up(r[g + "s1" + k][:, x], r[g + "rx" + k], nx - 1)
        r[g + "s2" + k][...] = total.astype(BF16)
        for i, device in enumerate(dev_y):
            send(g + "y" + k, i, r[g + "s2" + k].at[ys[i]], r[g + "ry" + k].at[i], device)

    def scatter_end(g, k):
        arrive(g + "y" + k)
        return add_up(r[g + "s2" + k][y], r[g + "ry" + k], ny - 1)

    def narrow_sum(g, k):
        for i, device in enumerate(dev_z):
            send(g + "rs" + k, i, r[g + "b" + k].at[zs[i]], r[g + "r" + k].at[i], device)

    def narrow_total(g, k):
        arrive(g + "rs" + k)
        return add_up(r[g + "b" + k][z], r[g + "r" + k], nz - 1)

    def narrow_hand(g, k):
        for i, device in enumerate(dev_z):
            send(g + "ag" + k, i, r[g + "g" + k].at[z], r[g + "g" + k].at[z], device)

    def small_row(g):
        for i, device in enumerate(dev_e):
            send(g + "e", i, r[g + "p"].at[es[i]], r[g + "re"].at[i], device)

    def small_y(g):
        arrive(g + "e")
        r[g + "s"][...] = add_up(r[g + "p"][e], r[g + "re"], ne - 1).astype(BF16)
        for i, device in enumerate(dev_y):
            send(g + "y", i, r[g + "s"], r[g + "ry"].at[i], device)

    def small_hand(g):
        arrive(g + "y")
        r[g + "f"][e] = add_up(r[g + "s"][...], r[g + "ry"], ny - 1).astype(BF16)
        for i, device in enumerate(dev_e):
            send(g + "E", i, r[g + "f"].at[e], r[g + "f"].at[e], device)

    rows = plan.bs * 16
    row = lax.broadcasted_iota(jnp.int32, (rows, rows), 0)
    col = lax.broadcasted_iota(jnp.int32, (rows, rows), 1)

    def by_block(v):
        return ((v >> 1) & 7) * (2 * plan.bs) + (v >> 4) * 2 + (v & 1)

    to_tokens = (row == by_block(col)).astype(F32).astype(BF16)
    to_shards = (col == by_block(row)).astype(F32).astype(BF16)

    def unpack(g, k, out, base):
        for b in range(plan.wide // plan.bs):
            block = r[g + "g" + k][plan.yb * b:plan.yb * (b + 1)].reshape(rows, LANES)
            turned = mm(to_tokens, block).astype(BF16)
            n = 2 * plan.bs
            for q in range(NQ):
                out[base + n * b:base + n * (b + 1), LANES * q:LANES * (q + 1)] = (
                    turned[n * q:n * (q + 1)])

    def pack(value, g, k):
        for b in range(plan.wide // plan.bs):
            n = 2 * plan.bs
            block = jnp.concatenate(
                [value[n * b:n * (b + 1), LANES * q:LANES * (q + 1)] for q in range(NQ)], axis=0)
            turned = mm(to_shards, block).astype(BF16)
            r[g + "r" + k][plan.yb * b:plan.yb * (b + 1)] = turned.reshape(
                plan.yb, nx, 2, 16, LANES)

    loads[0].wait()
    tok = r["tok"][...].astype(F32)
    for h in range(2):
        for q in range(NQ):
            r["t32"][h, 2 * q:2 * q + 2, :] = tok[2 * h:2 * h + 2, LANES * q:LANES * (q + 1)]
        r["Ag" + str(h)][y, x, c] = r["t32"][h].astype(BF16)

    lane = lax.broadcasted_iota(jnp.int32, (1, LANES), 1)
    mask = [token_mask[t].astype(F32) for t in range(4)]
    reward = [rewards[t] for t in range(4)]
    ids = [group_ids[t] for t in range(4)]
    reward_row = jnp.zeros((1, LANES), F32)
    count_row = jnp.zeros((1, LANES), F32)
    for t in range(4):
        reward_row += jnp.where(lane == ids[t], mask[t] * reward[t], 0.0)
        count_row += jnp.where(lane == ids[t], mask[t], 0.0)
    row8 = lax.broadcasted_iota(jnp.int32, (8, LANES), 0)
    r["st0"][...] = jnp.where(row8 == 0, reward_row, jnp.where(row8 == 1, count_row, 0.0))

    pl.semaphore_wait(barrier, len(peers))
    gather_y("A", "0")
    gather_y("A", "1")
    for i, device in enumerate(dev_e):
        send("ste_", i, r["st0"], r["ste"].at[i], device)
    loads[7].wait()
    cot = r["cot"][...].astype(F32)
    for h in range(2):
        for q in range(NQ):
            r["c32"][h, 2 * q:2 * q + 2, :] = cot[2 * h:2 * h + 2, LANES * q:LANES * (q + 1)]
    r["bd"][:RANK, fb:] = jnp.zeros((RANK, fb), BF16)
    r["bd"][RANK:, :fb] = jnp.zeros((RANK, fb), BF16)
    loads[0] = pltpu.make_async_copy(a_down, r["adown"], r["load"].at[0])
    loads[0].start()
    gather_x("A", "0")
    gather_x("A", "1")

    arrive("ste_")
    r["st1"][...] = add_up(r["st0"][...], r["ste"], ne - 1)
    for i, device in enumerate(dev_y):
        send("sty_", i, r["st1"], r["sty"].at[i], device)
    for i in (1, 2, 3, 4, 5, 6):
        loads[i].wait()
    gather_c("A", "0")
    gather_c("A", "1")

    def project(h):
        k = str(h)
        arrive("Ac" + k)
        unpack("A", k, r["x"], h * th)
        xv = r["x"][h * th:(h + 1) * th]
        r["Bb" + k][:, :, 2 * fb:] = (
            mm_nt(xv, r["agu"][...]).astype(BF16).reshape(nz, tz, LANES))
        r["Bb" + k][:, :, :2 * fb] = (
            mm(xv, r["wgu"][...]).astype(BF16).reshape(nz, tz, 2 * fb))
        narrow_sum("B", k)

    project(0)
    project(1)

    arrive("sty_")
    stats = add_up(r["st1"][...], r["sty"], ny - 1)
    group_count = stats[1:2]
    group_mean = stats[0:1] / jnp.maximum(group_count, 1.0)
    all_count = jnp.sum(group_count, axis=1, keepdims=True)
    scale_of = TOKENS / jnp.maximum(all_count, 1.0)
    advantage, token_scale = [], []
    for t in range(4):
        mean_t = jnp.sum(jnp.where(lane == ids[t], group_mean, 0.0), axis=1, keepdims=True)
        advantage.append(reward[t] - mean_t)
        token_scale.append(mask[t] * scale_of)
    loads[0].wait()

    def hidden(h):
        k = str(h)
        total = narrow_total("B", k)
        factors = total[:, 2 * fb:].astype(BF16)
        adapt = ADAPTER_SCALE * mm(factors, r["bd"][...])
        gate_base = total[:, :fb]
        up_base = total[:, fb:2 * fb]
        gate = gate_base + adapt[:, :fb]
        up = up_base + adapt[:, fb:]
        sig = jax.nn.sigmoid(gate)
        silu = gate * sig
        slope = sig * (1.0 + gate * (1.0 - sig))
        full = silu * up
        hp = full.astype(BF16)
        hd = (full - gate_base * jax.nn.sigmoid(gate_base) * up_base).astype(BF16)
        fd = ADAPTER_SCALE * mm_nt(hp, r["adown"][...])
        none = jnp.zeros_like(fd)
        fd = jnp.concatenate([none, fd] if h else [fd, none], axis=1)
        r["Hg" + k][z, :, :fb] = hd
        r["Hg" + k][z, :, fb:] = fd.astype(BF16)
        narrow_hand("H", k)
        r["Kg" + k][z, :, :fb] = (up * slope).astype(BF16)
        r["Kg" + k][z, :, fb:2 * fb] = silu.astype(BF16)
        r["Kg" + k][z, :, 2 * fb:3 * fb] = hp
        r["Kg" + k][z, :, 3 * fb:] = factors

    hidden(0)
    hidden(1)
    narrow_hand("K", "0")
    narrow_hand("K", "1")
    for i in (8, 9, 10):
        loads[i].wait()

    def outward(h):
        k = str(h)
        arrive("Hag" + k)
        both = r["Hg" + k][...].reshape(th, fb + LANES)
        pack(mm(both, r["downx"][...]).astype(BF16), "C", k)
        scatter_c("C", k)
        return both[:, fb:].astype(F32)

    row16 = lax.broadcasted_iota(jnp.int32, (16, 1), 0)
    even = (row16 & 1) == 0
    div = []

    def gradient(h):
        k = str(h)
        od = scatter_end("C", k)
        adv = jnp.where(even, advantage[2 * h], advantage[2 * h + 1])
        scl = jnp.where(even, token_scale[2 * h], token_scale[2 * h + 1])
        grad = scl * (KL_WEIGHT * od - adv * r["c32"][h])
        r["Dg" + k][y, x, c] = grad.astype(BF16)
        gather_y("D", k)
        square = od * od
        for t in range(2):
            picked = jnp.where(((row16 & 1) == t), square, 0.0)
            div.append(jnp.sum(jnp.sum(picked, axis=1, keepdims=True), axis=0, keepdims=True))

    fd0 = outward(0)
    scatter_x("C", "0")
    fd1 = outward(1)
    r["fdp"][...] = (fd0 + fd1).astype(BF16).reshape(ne, th // ne, LANES)
    small_row("fd")
    scatter_y("C", "0")
    scatter_x("C", "1")
    gradient(0)
    scatter_y("C", "1")
    small_y("fd")
    gather_x("D", "0")
    gradient(1)
    dv = jnp.zeros((8, LANES), F32)
    for t in range(4):
        dv += jnp.where(row8 == t, div[t], 0.0)
    r["dv"][...] = dv * (0.5 / D)
    for i, device in enumerate(dev_z):
        send("dv_", i, r["dv"], r["dvr"].at[i], device)
    gather_c("D", "0")
    gather_x("D", "1")
    small_hand("fd")

    def inward(h):
        k = str(h)
        arrive("Dc" + k)
        unpack("D", k, r["go" + k], 0)
        both = mm_nt(r["go" + k][...], r["downx"][...])
        gf = ADAPTER_SCALE * both[:, fb:]
        gh = both[:, :fb] + mm(gf[:, :RANK].astype(BF16), r["adown"][...])
        r["Eb" + k][...] = gh.astype(BF16).reshape(nz, tz, fb)
        narrow_sum("E", k)
        return gf

    gf0 = inward(0)
    gather_c("D", "1")
    gf1 = inward(1)
    r["Gb"][...] = jnp.where(lane < RANK, gf0, gf1).astype(BF16).reshape(nz, tz, LANES)
    for i, device in enumerate(dev_z):
        send("Grs", i, r["Gb"].at[zs[i]], r["Gr"].at[i], device)
    r["Eg0"][z] = narrow_total("E", "0").astype(BF16)
    narrow_hand("E", "0")
    arrive("fdE")
    fdf = r["fdf"][...].reshape(th, LANES)
    r["dog"][...] = mm_tn(fdf, r["go0"][...])[:RANK] + mm_tn(fdf, r["go1"][...])[RANK:]
    store(r["dog"], dog_o)
    r["Eg1"][z] = narrow_total("E", "1").astype(BF16)
    narrow_hand("E", "1")
    arrive("Grs")
    r["Gg"][z] = add_up(r["Gb"][z], r["Gr"], nz - 1).astype(BF16)
    for i, device in enumerate(dev_z):
        send("Gag", i, r["Gg"].at[z], r["Gg"].at[z], device)
    arrive("Kag0")
    arrive("Kag1")

    def back(h):
        k = str(h)
        arrive("Eag" + k)
        gh = r["Eg" + k][...].reshape(th, fb).astype(F32)
        kept = r["Kg" + k][...].reshape(th, 3 * fb + LANES)
        r["ggu" + k][:, :fb] = (gh * kept[:, :fb].astype(F32)).astype(BF16)
        r["ggu" + k][:, fb:] = (gh * kept[:, fb:2 * fb].astype(F32)).astype(BF16)
        ggu = r["ggu" + k][...]
        ad = (ADAPTER_SCALE * mm_nt(ggu, r["bd"][...])).astype(BF16)
        r["adp"][h * nx:(h + 1) * nx] = ad.reshape(nx, 2 * th // ne, LANES)
        if h == 1:
            small_row("ad")
        gx = mm_nt(ggu, r["wgu"][...]) + mm(ad, r["agu"][...])
        pack(gx.astype(BF16), "F", k)
        scatter_c("F", k)

    back(0)
    scatter_x("F", "0")
    back(1)
    scatter_y("F", "0")
    scatter_x("F", "1")
    small_y("ad")
    gu = jnp.zeros((LANES, 2 * fb), F32)
    for h in range(2):
        k = str(h)
        factors = r["Kg" + k][:, :, 3 * fb:].reshape(th, LANES)
        gu += mm_tn(factors, r["ggu" + k][...])
    r["gu"][...] = ADAPTER_SCALE * gu
    store(r["gu"].at[:RANK, :fb], gog_o)
    store(r["gu"].at[RANK:, fb:], uog_o)

    def input_gradient(h):
        gx = scatter_end("F", str(h))
        for q in range(NQ):
            r["o32"][2 * h:2 * h + 2, LANES * q:LANES * (q + 1)] = gx[2 * q:2 * q + 2]

    scatter_y("F", "1")
    small_hand("ad")
    input_gradient(0)
    arrive("Gag")
    gff = r["Gg"][...].reshape(th, LANES)
    parts = [mm_tn(gff, r["Kg" + k][:, :, 2 * fb:3 * fb].reshape(th, fb)) for k in "01"]
    r["gad"][...] = parts[0][:RANK] + parts[1][RANK:]
    store(r["gad"], gad_o)
    arrive("dv_")
    dv = add_up(r["dv"][...], r["dvr"], nz - 1)
    for t in range(4):
        dv_o[t] = jnp.max(dv[t:t + 1, :])
    input_gradient(1)
    r["gx"][...] = r["o32"][...].astype(BF16)
    store(r["gx"], gx_o)
    arrive("adE")
    r["gab"][...] = mm_tn(r["adf"][...].reshape(2 * th, LANES), r["x"][...])
    store(r["gab"].at[:RANK], ag_o)
    store(r["gab"].at[RANK:], au_o)

    for copy in pending:
        copy.wait_send()
    for copy in stores:
        copy.wait()


def finish_kernel(*refs):
    srcs, dsts, sems = refs[:8], refs[8:16], refs[16]
    copies = [pltpu.make_async_copy(srcs[i], dsts[i], sems.at[i]) for i in range(8)]
    for copy in copies:
        copy.start()
    for copy in copies:
        copy.wait()


def shards(wide, narrow, tokens, cotangent, rewards, group_ids, token_mask, w_gate, w_up, down_w,
           a_gate, a_up, gate_of, up_of, a_down, down_of):
    db, fb = w_gate.shape
    plan = Plan(wide, narrow, db, fb)
    hbm = pl.BlockSpec(memory_space=pltpu.HBM)
    sm = pl.BlockSpec(memory_space=pltpu.SMEM)
    s = jax.ShapeDtypeStruct
    shapes = (
        s((4, db), BF16), s((4,), F32), s((RANK, db), F32), s((RANK, db), F32),
        s((RANK, fb), F32), s((RANK, fb), F32), s((RANK, fb), F32), s((RANK, db), F32),
    )
    mids = pl.pallas_call(
        functools.partial(step_kernel, plan),
        out_shape=shapes,
        in_specs=[hbm, hbm, sm, sm, sm] + [hbm] * 9,
        out_specs=(hbm, sm) + (hbm,) * 6,
        scratch_shapes=plan.shapes,
        compiler_params=pltpu.CompilerParams(
            collective_id=0, has_side_effects=True, vmem_limit_bytes=60 << 20),
        name="policy_step",
    )(tokens, cotangent, rewards, group_ids, token_mask, w_gate, w_up, down_w, a_gate.T, a_up.T,
      gate_of, up_of, a_down.T, down_of)
    outs = pl.pallas_call(
        finish_kernel,
        out_shape=shapes,
        in_specs=[hbm] * 8,
        out_specs=(hbm,) * 8,
        scratch_shapes=[pltpu.SemaphoreType.DMA((8,))],
        compiler_params=pltpu.CompilerParams(vmem_limit_bytes=60 << 20),
        name="finish",
    )(*mids)
    gx, dv, ag, au, gog, uog, gad, dog = outs
    return gx, dv, ag.T, au.T, gog, uog, gad.T, dog


def solution(mesh):
    return jax.shard_map(
        functools.partial(shards, mesh.shape["wide"], mesh.shape["narrow"]),
        mesh=mesh,
        in_specs=(
            P("wide", "narrow"),
            P("wide", "narrow"),
            P("wide"),
            P("wide"),
            P("wide"),
            P("narrow", "wide"),
            P("narrow", "wide"),
            P("wide", "narrow"),
            P("narrow", None),
            P("narrow", None),
            P(None, "wide"),
            P(None, "wide"),
            P("wide", None),
            P(None, "narrow"),
        ),
        out_specs=(
            P("wide", "narrow"),
            P("wide"),
            P("narrow", None),
            P("narrow", None),
            P(None, "wide"),
            P(None, "wide"),
            P("wide", None),
            P(None, "narrow"),
        ),
        check_vma=False,
    )
```

time: 126 us -> 145 us (1.15)
  Pallas kernels: 116 us -> 144 us
  local copies, waits for them, and re-layouts: 9 us -> 0 us
    pallas_call x2, Pallas kernels: 116 us -> 144 us  [the longest x1 107 us: shards(): pl.pallas_call(functools.partial(step_kernel, plan), out_shape=shapes, in...]
    unnamed x29 -> x0, local copies, waits for them, and re-layouts: 6.46 us -> none
    pallas_call x3 -> x0, local copies, waits for them, and re-layouts: 2.55 us -> none  [shards(): pl.pallas_call(functools.partial(finish_kernel, fb), out_shape=(s((4, db)...]
where the time goes in v2:
time: 145 us
  Pallas kernels  144 us (99%)
    pallas_call x1, Pallas kernels, shards(): pl.pallas_call(functools.partial(step_kernel, plan), out_shape=shapes, in...  107 us
    pallas_call x1, Pallas kernels, shards(): pl.pallas_call(finish_kernel, out_shape=shapes, in_specs=[hbm] * 8, out_s...  37.2 us

profile of v2, /device:TPU:1, one launch (start us, length us, event | category | flops | bytes accessed | tf_op | source)
XLA Modules:
  0.0 144.6 jit_solution(16097089234585873578)
XLA Ops:
  0.6 106.8 %policy_step.1 = (bf16[4,1024]{1,0:T(4,128)(2,1)}, f32[4]{0:T(128)}, f32[64,1024]{1,0:T(8,128)}, f32[64,1024]{1,0:T(8,128)}, f32[64,512]{1,0:T(8,128)}, /*index=...) custom-call(bf16[4,1024]{1,0:T(4,128)(2,1)} %refs_0_.1, bf16[4,1024]{1,0:T(4,128)(2,1)} %refs_1_.1, f32[4]{0:T(128)} %refs_2_.1, ...), custom_call_target="tpu_custom_call" | custom-call | tf_op jit(solution)/shard_map/policy_step/pallas_call | solution.py:558
  107.5 37.2 %finish.1 = (bf16[4,1024]{1,0:T(4,128)(2,1)}, f32[4]{0:T(128)}, f32[64,1024]{1,0:T(8,128)}, f32[64,1024]{1,0:T(8,128)}, f32[64,512]{1,0:T(8,128)}, /*index=5*/f3...) custom-call(bf16[4,1024]{1,0:T(4,128)(2,1)} %get-tuple-element.24.refs_0_, f32[4]{0:T(128)} %get-tuple-element.25.refs_1_, ...), custom_call_target="tpu_custom_call" | custom-call | tf_op jit(solution)/shard_map/finish/pallas_call | solution.py:569

commit v3 on v2

--- a/solution.py
+++ b/solution.py
@@ -536,11 +536,15 @@
 
 
 def finish_kernel(*refs):
-    srcs, dsts, sems = refs[:8], refs[8:16], refs[16]
-    copies = [pltpu.make_async_copy(srcs[i], dsts[i], sems.at[i]) for i in range(8)]
-    for copy in copies:
+    srcs, dsts, held, sems = refs[:8], refs[8:16], refs[16:24], refs[24]
+    ins = [pltpu.make_async_copy(srcs[i], held[i], sems.at[i]) for i in range(8)]
+    outs = [pltpu.make_async_copy(held[i], dsts[i], sems.at[8 + i]) for i in range(8)]
+    for copy in ins:
         copy.start()
-    for copy in copies:
+    for i in range(8):
+        ins[i].wait()
+        outs[i].start()
+    for copy in outs:
         copy.wait()
 
 
@@ -571,7 +575,8 @@
         out_shape=shapes,
         in_specs=[hbm] * 8,
         out_specs=(hbm,) * 8,
-        scratch_shapes=[pltpu.SemaphoreType.DMA((8,))],
+        scratch_shapes=[pltpu.VMEM(v.shape, v.dtype) for v in shapes]
+        + [pltpu.SemaphoreType.DMA((16,))],
         compiler_params=pltpu.CompilerParams(vmem_limit_bytes=60 << 20),
         name="finish",
     )(*mids)

time: 145 us -> 110 us (0.76)
  Pallas kernels: 144 us -> 109 us
    pallas_call x1, Pallas kernels: 37.2 us -> 2.12 us  [shards(): pl.pallas_call(finish_kernel, out_shape=shapes, in_specs=[hbm] * 8, out_s...]
where the time goes in v3:
time: 110 us
  Pallas kernels  109 us (99%)
    pallas_call x1, Pallas kernels, shards(): pl.pallas_call(functools.partial(step_kernel, plan), out_shape=shapes, in...  107 us

profile of v3, /device:TPU:1, one launch (start us, length us, event | category | flops | bytes accessed | tf_op | source)
XLA Modules:
  0.0 109.6 jit_solution(16329509218818935693)
XLA Ops:
  0.6 106.8 %policy_step.1 = (bf16[4,1024]{1,0:T(4,128)(2,1)}, f32[4]{0:T(128)}, f32[64,1024]{1,0:T(8,128)}, f32[64,1024]{1,0:T(8,128)}, f32[64,512]{1,0:T(8,128)}, /*index=...) custom-call(bf16[4,1024]{1,0:T(4,128)(2,1)} %refs_0_.1, bf16[4,1024]{1,0:T(4,128)(2,1)} %refs_1_.1, f32[4]{0:T(128)} %refs_2_.1, ...), custom_call_target="tpu_custom_call" | custom-call | tf_op jit(solution)/shard_map/policy_step/pallas_call | solution.py:562
  107.5 2.1 %finish.1 = (bf16[4,1024]{1,0:T(4,128)(2,1)}, f32[4]{0:T(128)}, f32[64,1024]{1,0:T(8,128)}, f32[64,1024]{1,0:T(8,128)}, f32[64,512]{1,0:T(8,128)}, /*index=5*/f3...) custom-call(bf16[4,1024]{1,0:T(4,128)(2,1)} %get-tuple-element.24.refs_0_, f32[4]{0:T(128)} %get-tuple-element.25.refs_1_, ...), custom_call_target="tpu_custom_call" | custom-call | tf_op jit(solution)/shard_map/finish/pallas_call | solution.py:573

commit v4 on v3

--- a/solution.py
+++ b/solution.py
@@ -62,7 +62,7 @@
         v("gu", (LANES, 2 * fb), F32)
         v("gad", (RANK, fb), F32)
         v("dog", (RANK, db), F32)
-        self.dma("load", 11)
+        self.dma("load", 12)
         self.dma("out", 7)
         for h in range(2):
             k = str(h)
@@ -85,26 +85,38 @@
                 v(g + "b" + k, (nz, tz, width), BF16)
                 v(g + "r" + k, (nz - 1, tz, width), BF16)
                 self.rem(g + "rs" + k, nz - 1)
-            for g, width in (("H", fb + LANES), ("K", 3 * fb + LANES), ("E", fb)):
+            for g, width in (("H", fb + LANES), ("K", 2 * fb + LANES), ("E", fb)):
                 v(g + "g" + k, (nz, tz, width), BF16)
                 self.rem(g + "ag" + k, nz - 1)
+            v("hp" + k, (tz, fb), BF16)
             v("go" + k, (th, db), BF16)
             v("ggu" + k, (th, 2 * fb), BF16)
-        for g, rows in (("fd", th), ("ad", 2 * th)):
-            part = rows // ne
-            v(g + "p", (ne, part, LANES), BF16)
-            v(g + "re", (ne - 1, part, LANES), BF16)
-            v(g + "s", (part, LANES), BF16)
-            v(g + "ry", (ny - 1, part, LANES), BF16)
-            v(g + "f", (ne, part, LANES), BF16)
-            self.rem(g + "e", ne - 1)
-            self.rem(g + "y", ny - 1)
-            self.rem(g + "E", ne - 1)
+        part = th // ne
+        v("fdp", (ne, part, LANES), BF16)
+        v("fdre", (ne - 1, part, LANES), BF16)
+        v("fds", (part, LANES), BF16)
+        v("fdry", (ny - 1, part, LANES), BF16)
+        v("fdf", (ne, part, LANES), BF16)
+        self.rem("fde", ne - 1)
+        self.rem("fdy", ny - 1)
+        self.rem("fdE", ne - 1)
+        v("adp", (2, tz, LANES), BF16)
+        v("adre", (ne - 1, 2, tz, LANES), BF16)
+        v("ads", (2, tz, LANES), BF16)
+        v("adry", (ny - 1, 2, tz, LANES), BF16)
+        v("adf", (2, nz, tz, LANES), BF16)
+        self.rem("ade", ne - 1)
+        self.rem("ady", ny - 1)
+        self.rem("adz", nz - 1)
         v("Gb", (nz, tz, LANES), BF16)
         v("Gr", (nz - 1, tz, LANES), BF16)
-        v("Gg", (nz, tz, LANES), BF16)
         self.rem("Grs", nz - 1)
-        self.rem("Gag", nz - 1)
+        self.rb, self.cb = 2 * RANK // nz, fb // 2
+        v("Mb", (nz, self.rb, self.cb), BF16)
+        v("Mr", (nz - 1, self.rb, self.cb), BF16)
+        v("Mg", (nz, self.rb, self.cb), F32)
+        self.rem("Mrs", nz - 1)
+        self.rem("Mag", nz - 1)
         for name in ("st0", "st1", "dv"):
             v(name, (8, LANES), F32)
         v("ste", (ne - 1, 8, LANES), F32)
@@ -140,10 +152,13 @@
     e = w % ne
     other = 1 - c
 
-    ys = [(y + d) % ny for d in range(1, ny)]
-    xs = [(x + d) % nx for d in range(1, nx)]
-    es = [(e + d) % ne for d in range(1, ne)]
-    zs = [(z + d) % nz for d in range(1, nz)]
+    def far_first(n):
+        return sorted(range(1, n), key=lambda d: -min(d, n - d))
+
+    ys = [(y + d) % ny for d in far_first(ny)]
+    xs = [(x + d) % nx for d in far_first(nx)]
+    es = [((x + d) % nx) * 2 + v for d in far_first(nx) for v in (c, other)] + [x * 2 + other]
+    zs = [(z + d) % nz for d in far_first(nz)]
     dev_y = [(v * ne + e, z) for v in ys]
     dev_x = [(y * ne + v * 2 + c, z) for v in xs]
     dev_e = [(y * ne + v, z) for v in es]
@@ -156,16 +171,14 @@
         pl.semaphore_signal(barrier, inc=1, device_id=peer, device_id_type=MESH)
 
     loads = []
-    for src, dst in (
-        (tokens, r["tok"]), (w_gate, r["wgu"].at[:, :fb]), (w_up, r["wgu"].at[:, fb:]),
-        (a_gate, r["agu"].at[:RANK]), (a_up, r["agu"].at[RANK:]),
-        (gate_of, r["bd"].at[:RANK, :fb]), (up_of, r["bd"].at[RANK:, fb:]),
-        (cotangent, r["cot"]), (down_w, r["downx"].at[:fb]),
-        (down_of, r["downx"].at[fb:fb + RANK]), (down_of, r["downx"].at[fb + RANK:]),
-    ):
+
+    def load(src, dst):
         copy = pltpu.make_async_copy(src, dst, r["load"].at[len(loads)])
         copy.start()
         loads.append(copy)
+
+    load(tokens, r["tok"])
+    load(cotangent, r["cot"])
 
     pending = []
     flying = {}
@@ -185,6 +198,11 @@
         pending.append(copy)
         flying.setdefault(name, []).append(copy)
 
+    def settle():
+        for copy in pending:
+            copy.wait_send()
+        pending.clear()
+
     def arrive(name):
         for copy in flying.pop(name):
             copy.wait_recv()
@@ -260,34 +278,6 @@
         r[g + "f"][e] = add_up(r[g + "s"][...], r[g + "ry"], ny - 1).astype(BF16)
         for i, device in enumerate(dev_e):
             send(g + "E", i, r[g + "f"].at[e], r[g + "f"].at[e], device)
-
-    rows = plan.bs * 16
-    row = lax.broadcasted_iota(jnp.int32, (rows, rows), 0)
-    col = lax.broadcasted_iota(jnp.int32, (rows, rows), 1)
-
-    def by_block(v):
-        return ((v >> 1) & 7) * (2 * plan.bs) + (v >> 4) * 2 + (v & 1)
-
-    to_tokens = (row == by_block(col)).astype(F32).astype(BF16)
-    to_shards = (col == by_block(row)).astype(F32).astype(BF16)
-
-    def unpack(g, k, out, base):
-        for b in range(plan.wide // plan.bs):
-            block = r[g + "g" + k][plan.yb * b:plan.yb * (b + 1)].reshape(rows, LANES)
-            turned = mm(to_tokens, block).astype(BF16)
-            n = 2 * plan.bs
-            for q in range(NQ):
-                out[base + n * b:base + n * (b + 1), LANES * q:LANES * (q + 1)] = (
-                    turned[n * q:n * (q + 1)])
-
-    def pack(value, g, k):
-        for b in range(plan.wide // plan.bs):
-            n = 2 * plan.bs
-            block = jnp.concatenate(
-                [value[n * b:n * (b + 1), LANES * q:LANES * (q + 1)] for q in range(NQ)], axis=0)
-            turned = mm(to_shards, block).astype(BF16)
-            r[g + "r" + k][plan.yb * b:plan.yb * (b + 1)] = turned.reshape(
-                plan.yb, nx, 2, 16, LANES)
 
     loads[0].wait()
     tok = r["tok"][...].astype(F32)
@@ -313,15 +303,52 @@
     gather_y("A", "1")
     for i, device in enumerate(dev_e):
         send("ste_", i, r["st0"], r["ste"].at[i], device)
-    loads[7].wait()
+    load(w_gate, r["wgu"].at[:, :fb])
+    load(w_up, r["wgu"].at[:, fb:])
+    load(a_gate, r["agu"].at[:RANK])
+    load(a_up, r["agu"].at[RANK:])
+    load(gate_of, r["bd"].at[:RANK, :fb])
+    load(up_of, r["bd"].at[RANK:, fb:])
+    load(down_w, r["downx"].at[:fb])
+    load(down_of, r["downx"].at[fb:fb + RANK])
+    load(down_of, r["downx"].at[fb + RANK:])
+    load(a_down, r["adown"])
+
+    rows = plan.bs * 16
+    row = lax.broadcasted_iota(jnp.int32, (rows, rows), 0)
+    col = lax.broadcasted_iota(jnp.int32, (rows, rows), 1)
+
+    def by_block(v):
+        return ((v >> 1) & 7) * (2 * plan.bs) + (v >> 4) * 2 + (v & 1)
+
+    to_tokens = (row == by_block(col)).astype(F32).astype(BF16)
+    to_shards = (col == by_block(row)).astype(F32).astype(BF16)
+
+    def unpack(g, k, out, base):
+        for b in range(plan.wide // plan.bs):
+            block = r[g + "g" + k][plan.yb * b:plan.yb * (b + 1)].reshape(rows, LANES)
+            turned = mm(to_tokens, block).astype(BF16)
+            n = 2 * plan.bs
+            for q in range(NQ):
+                out[base + n * b:base + n * (b + 1), LANES * q:LANES * (q + 1)] = (
+                    turned[n * q:n * (q + 1)])
+
+    def pack(value, g, k):
+        for b in range(plan.wide // plan.bs):
+            n = 2 * plan.bs
+            block = jnp.concatenate(
+                [value[n * b:n * (b + 1), LANES * q:LANES * (q + 1)] for q in range(NQ)], axis=0)
+            turned = mm(to_shards, block).astype(BF16)
+            r[g + "r" + k][plan.yb * b:plan.yb * (b + 1)] = turned.reshape(
+                plan.yb, nx, 2, 16, LANES)
+
+    loads[1].wait()
     cot = r["cot"][...].astype(F32)
     for h in range(2):
         for q in range(NQ):
             r["c32"][h, 2 * q:2 * q + 2, :] = cot[2 * h:2 * h + 2, LANES * q:LANES * (q + 1)]
     r["bd"][:RANK, fb:] = jnp.zeros((RANK, fb), BF16)
     r["bd"][RANK:, :fb] = jnp.zeros((RANK, fb), BF16)
-    loads[0] = pltpu.make_async_copy(a_down, r["adown"], r["load"].at[0])
-    loads[0].start()
     gather_x("A", "0")
     gather_x("A", "1")
 
@@ -329,7 +356,7 @@
     r["st1"][...] = add_up(r["st0"][...], r["ste"], ne - 1)
     for i, device in enumerate(dev_y):
         send("sty_", i, r["st1"], r["sty"].at[i], device)
-    for i in (1, 2, 3, 4, 5, 6):
+    for i in range(2, 8):
         loads[i].wait()
     gather_c("A", "0")
     gather_c("A", "1")
@@ -359,7 +386,7 @@
         mean_t = jnp.sum(jnp.where(lane == ids[t], group_mean, 0.0), axis=1, keepdims=True)
         advantage.append(reward[t] - mean_t)
         token_scale.append(mask[t] * scale_of)
-    loads[0].wait()
+    loads[11].wait()
 
     def hidden(h):
         k = str(h)
@@ -384,14 +411,12 @@
         narrow_hand("H", k)
         r["Kg" + k][z, :, :fb] = (up * slope).astype(BF16)
         r["Kg" + k][z, :, fb:2 * fb] = silu.astype(BF16)
-        r["Kg" + k][z, :, 2 * fb:3 * fb] = hp
-        r["Kg" + k][z, :, 3 * fb:] = factors
+        r["Kg" + k][z, :, 2 * fb:] = factors
+        r["hp" + k][...] = hp
 
     hidden(0)
     hidden(1)
-    narrow_hand("K", "0")
-    narrow_hand("K", "1")
-    for i in (8, 9, 10):
+    for i in range(8, 11):
         loads[i].wait()
 
     def outward(h):
@@ -422,11 +447,14 @@
     fd0 = outward(0)
     scatter_x("C", "0")
     fd1 = outward(1)
+    settle()
+    narrow_hand("K", "0")
     r["fdp"][...] = (fd0 + fd1).astype(BF16).reshape(ne, th // ne, LANES)
     small_row("fd")
     scatter_y("C", "0")
     scatter_x("C", "1")
     gradient(0)
+    narrow_hand("K", "1")
     scatter_y("C", "1")
     small_y("fd")
     gather_x("D", "0")
@@ -440,6 +468,7 @@
     gather_c("D", "0")
     gather_x("D", "1")
     small_hand("fd")
+    settle()
 
     def inward(h):
         k = str(h)
@@ -458,47 +487,68 @@
     r["Gb"][...] = jnp.where(lane < RANK, gf0, gf1).astype(BF16).reshape(nz, tz, LANES)
     for i, device in enumerate(dev_z):
         send("Grs", i, r["Gb"].at[zs[i]], r["Gr"].at[i], device)
-    r["Eg0"][z] = narrow_total("E", "0").astype(BF16)
-    narrow_hand("E", "0")
+    def adapters(h):
+        k = str(h)
+        total = narrow_total("E", k).astype(BF16)
+        r["Eg" + k][z] = total
+        narrow_hand("E", k)
+        gh = total.astype(F32)
+        gate = (gh * r["Kg" + k][z, :, :fb].astype(F32)).astype(BF16)
+        up = (gh * r["Kg" + k][z, :, fb:2 * fb].astype(F32)).astype(BF16)
+        ad = mm_nt(gate, r["bd"][:, :fb]) + mm_nt(up, r["bd"][:, fb:])
+        r["adp"][h] = (ADAPTER_SCALE * ad).astype(BF16)
+
+    adapters(0)
+    adapters(1)
+    for i, device in enumerate(dev_e):
+        send("ade", i, r["adp"], r["adre"].at[i], device)
     arrive("fdE")
     fdf = r["fdf"][...].reshape(th, LANES)
     r["dog"][...] = mm_tn(fdf, r["go0"][...])[:RANK] + mm_tn(fdf, r["go1"][...])[RANK:]
     store(r["dog"], dog_o)
-    r["Eg1"][z] = narrow_total("E", "1").astype(BF16)
-    narrow_hand("E", "1")
     arrive("Grs")
-    r["Gg"][z] = add_up(r["Gb"][z], r["Gr"], nz - 1).astype(BF16)
+    gff = add_up(r["Gb"][z], r["Gr"], nz - 1).astype(BF16)
+    gad = mm_tn(gff, r["hp0"][...])[:RANK] + mm_tn(gff, r["hp1"][...])[RANK:]
+    rb, cb = plan.rb, plan.cb
+    for j in range(nz):
+        r["Mb"][j] = gad[j // 2 * rb:(j // 2 + 1) * rb, j % 2 * cb:(j % 2 + 1) * cb].astype(BF16)
     for i, device in enumerate(dev_z):
-        send("Gag", i, r["Gg"].at[z], r["Gg"].at[z], device)
+        send("Mrs", i, r["Mb"].at[zs[i]], r["Mr"].at[i], device)
     arrive("Kag0")
     arrive("Kag1")
+    settle()
 
     def back(h):
         k = str(h)
         arrive("Eag" + k)
         gh = r["Eg" + k][...].reshape(th, fb).astype(F32)
-        kept = r["Kg" + k][...].reshape(th, 3 * fb + LANES)
+        kept = r["Kg" + k][...].reshape(th, 2 * fb + LANES)
         r["ggu" + k][:, :fb] = (gh * kept[:, :fb].astype(F32)).astype(BF16)
         r["ggu" + k][:, fb:] = (gh * kept[:, fb:2 * fb].astype(F32)).astype(BF16)
         ggu = r["ggu" + k][...]
         ad = (ADAPTER_SCALE * mm_nt(ggu, r["bd"][...])).astype(BF16)
-        r["adp"][h * nx:(h + 1) * nx] = ad.reshape(nx, 2 * th // ne, LANES)
-        if h == 1:
-            small_row("ad")
         gx = mm_nt(ggu, r["wgu"][...]) + mm(ad, r["agu"][...])
         pack(gx.astype(BF16), "F", k)
         scatter_c("F", k)
 
     back(0)
+    arrive("ade")
+    r["ads"][...] = add_up(r["adp"][...], r["adre"], ne - 1).astype(BF16)
+    for i, device in enumerate(dev_y):
+        send("ady", i, r["ads"], r["adry"].at[i], device)
     scatter_x("F", "0")
     back(1)
     scatter_y("F", "0")
+    arrive("ady")
+    r["adf"][:, z] = add_up(r["ads"][...], r["adry"], ny - 1).astype(BF16)
+    for i, device in enumerate(dev_z):
+        send("adz", i, r["adf"].at[:, z], r["adf"].at[:, z], device)
     scatter_x("F", "1")
-    small_y("ad")
+    settle()
     gu = jnp.zeros((LANES, 2 * fb), F32)
     for h in range(2):
         k = str(h)
-        factors = r["Kg" + k][:, :, 3 * fb:].reshape(th, LANES)
+        factors = r["Kg" + k][:, :, 2 * fb:].reshape(th, LANES)
         gu += mm_tn(factors, r["ggu" + k][...])
     r["gu"][...] = ADAPTER_SCALE * gu
     store(r["gu"].at[:RANK, :fb], gog_o)
@@ -509,13 +559,19 @@
         for q in range(NQ):
             r["o32"][2 * h:2 * h + 2, LANES * q:LANES * (q + 1)] = gx[2 * q:2 * q + 2]
 
+    arrive("Mrs")
+    r["Mg"][z] = add_up(r["Mb"][z], r["Mr"], nz - 1)
+    for i, device in enumerate(dev_z):
+        send("Mag", i, r["Mg"].at[z], r["Mg"].at[z], device)
     scatter_y("F", "1")
-    small_hand("ad")
+    arrive("adz")
+    r["gab"][...] = mm_tn(r["adf"][...].reshape(2 * th, LANES), r["x"][...])
+    store(r["gab"].at[:RANK], ag_o)
+    store(r["gab"].at[RANK:], au_o)
     input_gradient(0)
-    arrive("Gag")
-    gff = r["Gg"][...].reshape(th, LANES)
-    parts = [mm_tn(gff, r["Kg" + k][:, :, 2 * fb:3 * fb].reshape(th, fb)) for k in "01"]
-    r["gad"][...] = parts[0][:RANK] + parts[1][RANK:]
+    arrive("Mag")
+    for j in range(nz):
+        r["gad"][j // 2 * rb:(j // 2 + 1) * rb, j % 2 * cb:(j % 2 + 1) * cb] = r["Mg"][j]
     store(r["gad"], gad_o)
     arrive("dv_")
     dv = add_up(r["dv"][...], r["dvr"], nz - 1)
@@ -524,13 +580,7 @@
     input_gradient(1)
     r["gx"][...] = r["o32"][...].astype(BF16)
     store(r["gx"], gx_o)
-    arrive("adE")
-    r["gab"][...] = mm_tn(r["adf"][...].reshape(2 * th, LANES), r["x"][...])
-    store(r["gab"].at[:RANK], ag_o)
-    store(r["gab"].at[RANK:], au_o)
-
-    for copy in pending:
-        copy.wait_send()
+    settle()
     for copy in stores:
         copy.wait()
 

time: 110 us -> 104 us (0.945)
  Pallas kernels: 109 us -> 103 us
    pallas_call x1, Pallas kernels: 107 us -> 101 us  [shards(): pl.pallas_call(functools.partial(step_kernel, plan), out_shape=shapes, in...]
where the time goes in v4:
time: 104 us; the launch traced here: 103 us
  Pallas kernels  103 us (99%)
    pallas_call x1, Pallas kernels, shards(): pl.pallas_call(functools.partial(step_kernel, plan), out_shape=shapes, in...  101 us
    pallas_call x1, Pallas kernels, shards(): pl.pallas_call(finish_kernel, out_shape=shapes, in_specs=[hbm] * 8, out_s...  2.12 us

profile of v4, /device:TPU:1, one launch (start us, length us, event | category | flops | bytes accessed | tf_op | source)
XLA Modules:
  0.0 103.4 jit_solution(18317619306318207535)
XLA Ops:
  0.6 100.6 %policy_step.1 = (bf16[4,1024]{1,0:T(4,128)(2,1)}, f32[4]{0:T(128)}, f32[64,1024]{1,0:T(8,128)}, f32[64,1024]{1,0:T(8,128)}, f32[64,512]{1,0:T(8,128)}, /*index=...) custom-call(bf16[4,1024]{1,0:T(4,128)(2,1)} %refs_0_.1, bf16[4,1024]{1,0:T(4,128)(2,1)} %refs_1_.1, f32[4]{0:T(128)} %refs_2_.1, ...), custom_call_target="tpu_custom_call" | custom-call | tf_op jit(solution)/shard_map/policy_step/pallas_call | solution.py:612
  101.3 2.1 %finish.1 = (bf16[4,1024]{1,0:T(4,128)(2,1)}, f32[4]{0:T(128)}, f32[64,1024]{1,0:T(8,128)}, f32[64,1024]{1,0:T(8,128)}, f32[64,512]{1,0:T(8,128)}, /*index=5*/f3...) custom-call(bf16[4,1024]{1,0:T(4,128)(2,1)} %get-tuple-element.24.refs_0_, f32[4]{0:T(128)} %get-tuple-element.25.refs_1_, ...), custom_call_target="tpu_custom_call" | custom-call | tf_op jit(solution)/shard_map/finish/pallas_call | solution.py:623

commit v5 on v4

--- a/solution.py
+++ b/solution.py
@@ -48,6 +48,8 @@
         v = self.vmem
         v("wgu", (db, 2 * fb), BF16)
         v("downx", (fb + LANES, db), BF16)
+        v("wgt", (2 * fb, db), BF16)
+        v("dnt", (db, fb + LANES), BF16)
         v("agu", (LANES, db), BF16)
         v("bd", (LANES, 2 * fb), BF16)
         v("adown", (RANK, fb), BF16)
@@ -85,6 +87,12 @@
                 v(g + "b" + k, (nz, tz, width), BF16)
                 v(g + "r" + k, (nz - 1, tz, width), BF16)
                 self.rem(g + "rs" + k, nz - 1)
+            v("Bl" + k, (tz, fb), BF16)
+            v("Bu" + k, (tz, fb + LANES), BF16)
+            v("Bq" + k, (2, tz, 2 * fb + LANES), BF16)
+            v("Bc" + k, (2, tz, 2 * fb + LANES), BF16)
+            for g, count in (("Bl", 1), ("Bu", 1), ("Bq", 2), ("Bd", 2), ("Bc", 2)):
+                self.rem(g + k, count)
             for g, width in (("H", fb + LANES), ("K", 2 * fb + LANES), ("E", fb)):
                 v(g + "g" + k, (nz, tz, width), BF16)
                 self.rem(g + "ag" + k, nz - 1)
@@ -259,6 +267,48 @@
         arrive(g + "rs" + k)
         return add_up(r[g + "b" + k][z], r[g + "r" + k], nz - 1)
 
+    def at_z(d):
+        return (z + d + nz) % nz
+
+    def dev_at(d):
+        return (w, at_z(d))
+
+    def ring_sum(k):
+        if nz != 8:
+            narrow_sum("B", k)
+            return
+        b = r["Bb" + k]
+        send("Bl" + k, 0, b.at[at_z(4), :, :fb], r["Bl" + k], dev_at(2))
+        send("Bu" + k, 0, b.at[at_z(4), :, fb:], r["Bu" + k], dev_at(-2))
+        for i, sign in enumerate((1, -1)):
+            send("Bq" + k, i, b.at[at_z(3 * sign)], r["Bq" + k].at[i], dev_at(sign))
+        for i, sign in enumerate((1, -1)):
+            send("Bd" + k, i, b.at[at_z(sign)], r["Br" + k].at[i], dev_at(sign))
+
+    def ring_relay(k):
+        if nz != 8:
+            return
+        b = r["Bb" + k]
+        for name in ("Bl", "Bu", "Bq"):
+            arrive(name + k)
+        for i, sign in enumerate((1, -1)):
+            both = b[at_z(2 * sign)].astype(F32) + r["Bq" + k][i].astype(F32)
+            low, high = both[:, :fb], both[:, fb:]
+            if i == 0:
+                low += r["Bl" + k][...].astype(F32)
+            else:
+                high += r["Bu" + k][...].astype(F32)
+            r["Bc" + k][i, :, :fb] = low.astype(BF16)
+            r["Bc" + k][i, :, fb:] = high.astype(BF16)
+            send("Bc" + k, i, r["Bc" + k].at[i], r["Br" + k].at[2 + i], dev_at(2 * sign))
+
+    def ring_total(k):
+        if nz != 8:
+            return narrow_total("B", k)
+        arrive("Bd" + k)
+        arrive("Bc" + k)
+        return add_up(r["Bb" + k][z], r["Br" + k], 4)
+
     def narrow_hand(g, k):
         for i, device in enumerate(dev_z):
             send(g + "ag" + k, i, r[g + "g" + k].at[z], r[g + "g" + k].at[z], device)
@@ -370,10 +420,16 @@
             mm_nt(xv, r["agu"][...]).astype(BF16).reshape(nz, tz, LANES))
         r["Bb" + k][:, :, :2 * fb] = (
             mm(xv, r["wgu"][...]).astype(BF16).reshape(nz, tz, 2 * fb))
-        narrow_sum("B", k)
+        ring_sum(k)
+
+    def turn(src, dst, begin, end):
+        for i in range(begin, end, db // 8):
+            dst[:, i:i + db // 8] = src[i:i + db // 8, :].T
 
     project(0)
     project(1)
+    turn(r["wgu"], r["wgt"], 0, db // 2)
+    ring_relay("0")
 
     arrive("sty_")
     stats = add_up(r["st1"][...], r["sty"], ny - 1)
@@ -387,10 +443,12 @@
         advantage.append(reward[t] - mean_t)
         token_scale.append(mask[t] * scale_of)
     loads[11].wait()
+    ring_relay("1")
+    turn(r["wgu"], r["wgt"], db // 2, db)
 
     def hidden(h):
         k = str(h)
-        total = narrow_total("B", k)
+        total = ring_total(k)
         factors = total[:, 2 * fb:].astype(BF16)
         adapt = ADAPTER_SCALE * mm(factors, r["bd"][...])
         gate_base = total[:, :fb]
@@ -418,6 +476,7 @@
     hidden(1)
     for i in range(8, 11):
         loads[i].wait()
+    turn(r["downx"], r["dnt"], 0, fb + LANES)
 
     def outward(h):
         k = str(h)
@@ -474,7 +533,7 @@
         k = str(h)
         arrive("Dc" + k)
         unpack("D", k, r["go" + k], 0)
-        both = mm_nt(r["go" + k][...], r["downx"][...])
+        both = mm(r["go" + k][...], r["dnt"][...])
         gf = ADAPTER_SCALE * both[:, fb:]
         gh = both[:, :fb] + mm(gf[:, :RANK].astype(BF16), r["adown"][...])
         r["Eb" + k][...] = gh.astype(BF16).reshape(nz, tz, fb)
@@ -527,7 +586,7 @@
         r["ggu" + k][:, fb:] = (gh * kept[:, fb:2 * fb].astype(F32)).astype(BF16)
         ggu = r["ggu" + k][...]
         ad = (ADAPTER_SCALE * mm_nt(ggu, r["bd"][...])).astype(BF16)
-        gx = mm_nt(ggu, r["wgu"][...]) + mm(ad, r["agu"][...])
+        gx = mm(ggu, r["wgt"][...]) + mm(ad, r["agu"][...])
         pack(gx.astype(BF16), "F", k)
         scatter_c("F", k)
 

time: 104 us -> 101 us (0.971)
  Pallas kernels: 103 us -> 99.8 us
    pallas_call x1, Pallas kernels: 101 us -> 97.6 us  [shards(): pl.pallas_call(functools.partial(step_kernel, plan), out_shape=shapes, in...]
where the time goes in v5:
time: 101 us; the launch traced here: 100 us
  Pallas kernels  99.8 us (99%)
    pallas_call x1, Pallas kernels, shards(): pl.pallas_call(functools.partial(step_kernel, plan), out_shape=shapes, in...  97.6 us
    pallas_call x1, Pallas kernels, shards(): pl.pallas_call(finish_kernel, out_shape=shapes, in_specs=[hbm] * 8, out_s...  2.12 us

profile of v5, /device:TPU:1, one launch (start us, length us, event | category | flops | bytes accessed | tf_op | source)
XLA Modules:
  0.0 100.4 jit_solution(10814809070526275544)
XLA Ops:
  0.6 97.6 %policy_step.1 = (bf16[4,1024]{1,0:T(4,128)(2,1)}, f32[4]{0:T(128)}, f32[64,1024]{1,0:T(8,128)}, f32[64,1024]{1,0:T(8,128)}, f32[64,512]{1,0:T(8,128)}, /*index=...) custom-call(bf16[4,1024]{1,0:T(4,128)(2,1)} %refs_0_.1, bf16[4,1024]{1,0:T(4,128)(2,1)} %refs_1_.1, f32[4]{0:T(128)} %refs_2_.1, ...), custom_call_target="tpu_custom_call" | custom-call | tf_op jit(solution)/shard_map/policy_step/pallas_call | solution.py:671
  98.3 2.1 %finish.1 = (bf16[4,1024]{1,0:T(4,128)(2,1)}, f32[4]{0:T(128)}, f32[64,1024]{1,0:T(8,128)}, f32[64,1024]{1,0:T(8,128)}, f32[64,512]{1,0:T(8,128)}, /*index=5*/f3...) custom-call(bf16[4,1024]{1,0:T(4,128)(2,1)} %get-tuple-element.24.refs_0_, f32[4]{0:T(128)} %get-tuple-element.25.refs_1_, ...), custom_call_target="tpu_custom_call" | custom-call | tf_op jit(solution)/shard_map/finish/pallas_call | solution.py:682

commit v6 on v5

--- a/solution.py
+++ b/solution.py
@@ -206,10 +206,10 @@
         pending.append(copy)
         flying.setdefault(name, []).append(copy)
 
-    def settle():
-        for copy in pending:
+    def settle(keep=0):
+        for copy in pending[:len(pending) - keep]:
             copy.wait_send()
-        pending.clear()
+        del pending[:len(pending) - keep]
 
     def arrive(name):
         for copy in flying.pop(name):
@@ -506,7 +506,7 @@
     fd0 = outward(0)
     scatter_x("C", "0")
     fd1 = outward(1)
-    settle()
+    settle(20)
     narrow_hand("K", "0")
     r["fdp"][...] = (fd0 + fd1).astype(BF16).reshape(ne, th // ne, LANES)
     small_row("fd")
@@ -527,7 +527,7 @@
     gather_c("D", "0")
     gather_x("D", "1")
     small_hand("fd")
-    settle()
+    settle(20)
 
     def inward(h):
         k = str(h)
@@ -575,7 +575,7 @@
         send("Mrs", i, r["Mb"].at[zs[i]], r["Mr"].at[i], device)
     arrive("Kag0")
     arrive("Kag1")
-    settle()
+    settle(28)
 
     def back(h):
         k = str(h)
@@ -603,7 +603,7 @@
     for i, device in enumerate(dev_z):
         send("adz", i, r["adf"].at[:, z], r["adf"].at[:, z], device)
     scatter_x("F", "1")
-    settle()
+    settle(20)
     gu = jnp.zeros((LANES, 2 * fb), F32)
     for h in range(2):
         k = str(h)

time: 101 us -> 98.4 us (0.974)
  Pallas kernels: 99.8 us -> 97.5 us
    pallas_call x1, Pallas kernels: 97.6 us -> 95.4 us  [shards(): pl.pallas_call(functools.partial(step_kernel, plan), out_shape=shapes, in...]
where the time goes in v6:
time: 98.4 us; the launch traced here: 98.2 us
  Pallas kernels  97.5 us (99%)
    pallas_call x1, Pallas kernels, shards(): pl.pallas_call(functools.partial(step_kernel, plan), out_shape=shapes, in...  95.4 us
    pallas_call x1, Pallas kernels, shards(): pl.pallas_call(finish_kernel, out_shape=shapes, in_specs=[hbm] * 8, out_s...  2.12 us

profile of v6, /device:TPU:1, one launch (start us, length us, event | category | flops | bytes accessed | tf_op | source)
XLA Modules:
  0.0 98.2 jit_solution(6347032947140965079)
XLA Ops:
  0.6 95.4 %policy_step.1 = (bf16[4,1024]{1,0:T(4,128)(2,1)}, f32[4]{0:T(128)}, f32[64,1024]{1,0:T(8,128)}, f32[64,1024]{1,0:T(8,128)}, f32[64,512]{1,0:T(8,128)}, /*index=...) custom-call(bf16[4,1024]{1,0:T(4,128)(2,1)} %refs_0_.1, bf16[4,1024]{1,0:T(4,128)(2,1)} %refs_1_.1, f32[4]{0:T(128)} %refs_2_.1, ...), custom_call_target="tpu_custom_call" | custom-call | tf_op jit(solution)/shard_map/policy_step/pallas_call | solution.py:671
  96.1 2.1 %finish.1 = (bf16[4,1024]{1,0:T(4,128)(2,1)}, f32[4]{0:T(128)}, f32[64,1024]{1,0:T(8,128)}, f32[64,1024]{1,0:T(8,128)}, f32[64,512]{1,0:T(8,128)}, /*index=5*/f3...) custom-call(bf16[4,1024]{1,0:T(4,128)(2,1)} %get-tuple-element.24.refs_0_, f32[4]{0:T(128)} %get-tuple-element.25.refs_1_, ...), custom_call_target="tpu_custom_call" | custom-call | tf_op jit(solution)/shard_map/finish/pallas_call | solution.py:682
